TPU v7x, 512 devices: a whole 4x4x16 slice. The times are simulated.
512 devices in a mesh: row: 16 (over x, z_lo), col: 32 (over y, z_hi, core).
Axes of the slice: x: 4, y: 4, z: 16 (z_hi: 4, z_lo: 4; z = z_hi * 4 + z_lo), core: 2. Of those that a mesh axis runs over, the one named last changes fastest.
Arguments:
- layer_input: bfloat16 [2560, 8192], P('col', 'row'), may hold values from -6 to 6
- w_query: bfloat16 [8192, 8192], P('row', 'col'), may hold values from -0.0625 to 0.0625
- w_key: bfloat16 [8192, 1024], P('row', 'col'), may hold values from -0.0625 to 0.0625
- w_value: bfloat16 [8192, 1024], P('row', 'col'), may hold values from -0.0625 to 0.0625
- rotated_query_state: bfloat16 [2560, 8192], P('row', 'col'), may hold values from -156 to 156
- rotated_key_state: bfloat16 [2560, 1024], P('row', 'col'), may hold values from -6 to 6
- saved_value_state: bfloat16 [2560, 1024], P('row', 'col'), may hold values from -6 to 6
- context_gradient: bfloat16 [2560, 8192], P('row', 'col'), may hold values from -24 to 24
- positions: int32 [2560], P('row'), may hold values from 0 to 1982, as said below
- segment_ids: int32 [2560], P('row'), may hold values from 0 to 1, as said below
Outputs:
- grad_input: bfloat16 [2560, 8192], P('col', 'row')
- grad_wq: float32 [8192, 8192], P('row', 'col')
- grad_wk: float32 [8192, 1024], P('row', 'col')
- grad_wv: float32 [8192, 1024], P('row', 'col')
Inputs may be any that keep to these rules, and one draw needn't show every extreme that they name: `segment_ids`: never falls along the tokens; each of the 2 rollouts holds at least one token. `positions`: rises by one from each token to the next within a rollout.
All inputs are finite; a program needn't handle non-finite values.
Results may differ from a plain program's by a relative error of at most 0.025.
Values may be sent and summed in bfloat16 or wider, within the bound.
A program may use at most 64 MiB of HBM per device.

v0:
```python
import math

import jax
import jax.numpy as jnp
from jax import lax
from jax.sharding import PartitionSpec as P

KEY_VALUE_HEADS = 8
HEAD_SIZE = 128


rope_base = 500000.0


def partner_2(value, axis, apart):
    mask = 2**apart
    pairs = [(source, source ^ mask) for source in range(lax.axis_size(axis))]
    return lax.ppermute(value, axis, pairs)


def contract(left, right, left_dim, right_dim):
    return lax.dot_general(
        left, right, (((left_dim,), (right_dim,)), ((), ())), preferred_element_type=jnp.float32
    )


def rope_tables(positions):
    half_width = HEAD_SIZE // 2
    freq = jnp.exp(
        -(2.0 * jnp.arange(half_width, dtype=jnp.float32) / HEAD_SIZE) * math.log(rope_base)
    )
    angle = positions.astype(jnp.float32)[:, None] * freq[None, :]
    return (jnp.cos(angle), jnp.sin(angle))


def unrotate(gradient, cosine, sine):
    half_width = gradient.shape[-1] // 2
    first = gradient[..., :half_width]
    second = gradient[..., half_width:]
    return jnp.concatenate(
        [first * cosine + second * sine, second * cosine - first * sine], axis=-1
    )


def join_halves(mine, partner, bit_level, col_index):
    upper_bit = col_index >> bit_level & 1
    low_first = jnp.concatenate([mine, partner], axis=2)
    high_first = jnp.concatenate([partner, mine], axis=2)
    return jnp.where(upper_bit == 0, low_first, high_first)


def head_rows(states, head_count):
    count_rows = states.shape[0]
    return (
        states.reshape(count_rows, head_count, HEAD_SIZE)
        .transpose(1, 0, 2)
        .reshape(head_count * count_rows, HEAD_SIZE)
    )


def shards(
    layer_input,
    w_query,
    w_key,
    w_value,
    rotated_query_state,
    rotated_key_state,
    saved_value_state,
    context_gradient,
    positions,
    segment_ids,
):
    score_scale = HEAD_SIZE ** (-0.5)
    local_tokens = rotated_query_state.shape[0]
    head_count = rotated_query_state.shape[1] // HEAD_SIZE
    shared_heads = lax.axis_size("col") // KEY_VALUE_HEADS
    levels = shared_heads.bit_length() - 1
    col_index = lax.axis_index("col")
    labels = lax.all_gather(jnp.stack([positions, segment_ids]), "row", axis=1, tiled=True)
    key_count = labels.shape[1]
    visible = (segment_ids[:, None] == labels[1][None, :]) & (
        labels[0][None, :] <= positions[:, None]
    )
    key_pair = jnp.stack([rotated_key_state, saved_value_state], axis=1)
    key_pair = lax.all_gather(key_pair, "row", axis=0, tiled=True)
    for bit_level in range(levels):
        partner = partner_2(key_pair, "col", bit_level)
        key_pair = join_halves(key_pair, partner, bit_level, col_index)
    key_full = key_pair[:, 0]
    value_full = key_pair[:, 1]
    query_rows = head_rows(rotated_query_state, head_count)
    grad_rows = head_rows(context_gradient, head_count)
    scores = (contract(query_rows, key_full, 1, 1) * score_scale).reshape(
        head_count, local_tokens, key_count
    )
    row_peak = jnp.max(jnp.where(visible[None], scores, -1e30), axis=-1, keepdims=True)
    exponent_terms = jnp.where(visible[None], jnp.exp(scores - row_peak), 0.0)
    row_total = jnp.sum(exponent_terms, axis=-1, keepdims=True)
    weights = exponent_terms / row_total
    dweights = contract(grad_rows, value_full, 1, 1).reshape(head_count, local_tokens, key_count)
    row_delta = jnp.sum(weights * dweights, axis=-1, keepdims=True)
    dscores = (weights * (dweights - row_delta) * score_scale).astype(jnp.bfloat16)
    flat_dscores = dscores.reshape(head_count * local_tokens, key_count)
    dquery_rot = (
        contract(flat_dscores, key_full, 1, 0)
        .reshape(head_count, local_tokens, HEAD_SIZE)
        .transpose(1, 0, 2)
    )
    cosine, sine = rope_tables(positions)
    dquery = (
        unrotate(dquery_rot, cosine[:, None], sine[:, None])
        .reshape(local_tokens, head_count * HEAD_SIZE)
        .astype(jnp.bfloat16)
    )
    weights_low = weights.astype(jnp.bfloat16).reshape(head_count * local_tokens, key_count)
    dkey_part = contract(flat_dscores, query_rows, 0, 0)
    dvalue_part = contract(weights_low, grad_rows, 0, 0)
    pair_grads = lax.psum_scatter(
        jnp.stack([dkey_part, dvalue_part], axis=1).astype(jnp.bfloat16),
        "row",
        scatter_dimension=0,
        tiled=True,
    ).astype(jnp.float32)
    key_unrotated = unrotate(pair_grads[:, 0], cosine, sine)
    pair_grads = jnp.stack([key_unrotated, pair_grads[:, 1]], axis=1)
    for bit_level in reversed(range(levels)):
        half_width = pair_grads.shape[2] // 2
        upper_bit = col_index >> bit_level & 1
        lower_part = pair_grads[:, :, :half_width]
        upper_part = pair_grads[:, :, half_width:]
        kept_half = jnp.where(upper_bit == 0, lower_part, upper_part)
        sent_half = jnp.where(upper_bit == 0, upper_part, lower_part)
        pair_grads = kept_half + partner_2(sent_half.astype(jnp.bfloat16), "col", bit_level).astype(
            sent_half.dtype
        )
    local_grads = jnp.concatenate(
        [dquery, pair_grads[:, 0].astype(jnp.bfloat16), pair_grads[:, 1].astype(jnp.bfloat16)],
        axis=1,
    )
    grads_full = lax.all_gather(local_grads, "row", axis=0, tiled=True)
    weights_all = jnp.concatenate([w_query, w_key, w_value], axis=1)
    matching = grads_full
    weight_grads = contract(lax.all_gather(layer_input, "col", axis=0, tiled=True), matching, 0, 0)
    matching = grads_full
    grad_input = lax.psum_scatter(
        contract(matching, weights_all, 1, 1).astype(jnp.bfloat16),
        "col",
        scatter_dimension=0,
        tiled=True,
    )
    query_cols = w_query.shape[1]
    key_cols = w_key.shape[1]
    grad_wq = weight_grads[:, :query_cols]
    grad_wk = weight_grads[:, query_cols : query_cols + key_cols]
    grad_wv = weight_grads[:, query_cols + key_cols :]
    return (grad_input, grad_wq, grad_wk, grad_wv)


def solution(mesh):
    return jax.shard_map(
        shards,
        mesh=mesh,
        in_specs=(
            P("col", "row"),
            P("row", "col"),
            P("row", "col"),
            P("row", "col"),
            P("row", "col"),
            P("row", "col"),
            P("row", "col"),
            P("row", "col"),
            P("row"),
            P("row"),
        ),
        out_specs=(P("col", "row"), P("row", "col"), P("row", "col"), P("row", "col")),
        check_vma=False,
    )
```

profile of v0, /device:TPU:1, one launch (start us, length us, event | category | flops | bytes accessed | tf_op | source)
XLA Modules:
  0.0 601.1 jit_solution(2764270492980729466)
XLA Ops:
  7.2 0.0 reduce-scatter.3.cloned.1.call-start
  7.3 0.8 pad_maximum_fusion.3
  8.0 0.1 copy.30
  8.2 52.0 %all_gather.13 = bf16[2560,2,32]{2,0,1:T(8,128)(2,1)S(1)} all-gather(bf16[160,2,32]{2,0,1:T(8,128)(2,1)S(1)} %copy.30), channel_id=1, replica_groups=mesh['row'=16,'col'=32] {'row'}, dimensions={0}, use_global_device_ids=true | all-gather | bytes 348160 | tf_op jit(solution)/shard_map/all_gather | solution.py:85
  60.2 0.5 copy.31
  60.7 9.2 %collective-permute-start = (bf16[2560,2,32]{0,2,1:T(8,128)(2,1)S(1)}, bf16[2560,2,32]{0,2,1:T(8,128)(2,1)S(1)}, u32[]{:S(2)}, u32[]{:S(2)}) collective-permute-start(bf16[2560,2,32]{0,2,1:T(8,128)(2,1)S(1)} %copy.31), channel_id=1, source_target_pairs={{0,1},{1,0},{2,3},{3,2},{4,5},{5,4},{6,7},{7,6},{8,9},{9,8},{10,11... | collective-permute-start | bytes 983048 | tf_op jit(solution)/shard_map/ppermute | solution.py:18
  70.0 30.0 %all-gather = s32[16,160,2]{1,2,0:T(2,128)S(1)} all-gather(s32[1,160,2]{1,2,0:T(2,128)S(1)} %add_bitcast_fusion), channel_id=1, replica_groups=mesh['row'=16,'col'=32] {'row'}, dimensions={0}, use_global_device_ids=true | all-gather | bytes 21760 | tf_op jit(solution)/shard_map/all_gather | solution.py:79
  100.0 0.1 reshape.175
  100.1 0.1 slice_reduce_fusion.1
  100.2 1.4 copy.32
  101.6 3.2 maximum_select_fusion
  104.8 0.6 copy.34
  105.4 9.8 %collective-permute-start.1 = (bf16[2560,2,64]{0,2,1:T(8,128)(2,1)S(1)}, bf16[2560,2,64]{0,2,1:T(8,128)(2,1)}, u32[]{:S(2)}, u32[]{:S(2)}) collective-permute-start(bf16[2560,2,64]{0,2,1:T(8,128)(2,1)S(1)} %copy.34), channel_id=1, source_target_pairs={{0,2},{1,3},{2,0},{3,1},{4,6},{5,7},{6,4},{7,5},{8,10},{9,11},{10,... | collective-permute-start | bytes 1966088 | tf_op jit(solution)/shard_map/ppermute | solution.py:18
  115.2 0.4 compare_and_fusion
  115.6 54.1 %collective-permute-done.1 = bf16[2560,2,64]{0,2,1:T(8,128)(2,1)} collective-permute-done((bf16[2560,2,64]{0,2,1:T(8,128)(2,1)S(1)}, bf16[2560,2,64]{0,2,1:T(8,128)(2,1)}, u32[]{:S(2)}, u32[]{:S(2)}) %collective-permute-start.1) | collective-permute-done | bytes 655392 | tf_op jit(solution)/shard_map/ppermute | solution.py:18
  169.8 1.6 copy.35
  171.4 1.4 maximum_select_fusion.1
  172.9 0.2 broadcast_in_dim.33
  173.1 1.1 copy-done.4
  174.2 0.9 fusion.8
  175.1 0.1 sub.43
  175.2 2.7 fusion.12
  177.8 0.1 div.26
  177.9 3.1 fusion.11
  181.0 2.3 fusion.4
  183.3 0.1 sub.46
  183.4 3.3 fusion.2
  186.7 0.7 copy-done.3
  187.4 1.7 fusion.3
  189.1 1.2 pad_maximum_fusion
  190.2 0.0 reduce-scatter.3.cloned.1.call-update
  190.3 0.2 all-gather.4.cloned.1.call-start
  190.5 2.5 fusion.7
  193.0 0.6 convolution_bitcast_fusion.3
  193.6 75.5 %reduce-scatter.3.cloned.1.call-done = bf16[160,2,128]{2,0,1:T(8,128)(2,1)} async-done(((bf16[2560,2,128]{2,0,1:T(8,128)(2,1)}), bf16[160,2,128]{2,0,1:T(8,128)(2,1)}) %reduce-scatter.3.cloned.1.call-update) | async-done | bytes 81936 | tf_op jit(solution)/shard_map/reduce_scatter | solution.py:118
  269.2 0.9 convert_element_type.48
  270.1 0.4 multiply_cosine_fusion
  270.5 0.1 maximum_bitcast_fusion.1
  270.6 0.8 slice.93
  271.4 0.1 select_convert_fusion.1
  271.4 7.4 %collective-permute-start.2 = (bf16[160,2,64]{2,0,1:T(8,128)(2,1)S(1)}, bf16[160,2,64]{2,0,1:T(8,128)(2,1)S(1)}, u32[]{:S(2)}, u32[]{:S(2)}) collective-permute-start(bf16[160,2,64]{2,0,1:T(8,128)(2,1)S(1)} %select_convert_fusion.1), channel_id=1, source_target_pairs={{0,2},{1,3},{2,0},{3,1},{4,6},{5,7},{6,4},{7,5},{8,10},{9,11},{10,... | collective-permute-start | bytes 122888 | tf_op jit(solution)/shard_map/ppermute | solution.py:18
  278.9 0.1 add_convert_fusion.1
  279.0 1.7 collective-permute-done.2
  280.7 0.1 convert_add_fusion
  280.8 0.1 select_convert_fusion
  280.9 14.4 %collective-permute-start.3 = (bf16[160,2,32]{2,0,1:T(8,128)(2,1)S(1)}, bf16[160,2,32]{2,0,1:T(8,128)(2,1)S(1)}, u32[]{:S(2)}, u32[]{:S(2)}) collective-permute-start(bf16[160,2,32]{2,0,1:T(8,128)(2,1)S(1)} %select_convert_fusion), channel_id=1, source_target_pairs={{0,1},{1,0},{2,3},{3,2},{4,5},{5,4},{6,7},{7,6},{8,9},{9,8},{10,11... | collective-permute-start | bytes 61448 | tf_op jit(solution)/shard_map/ppermute | solution.py:18
  295.3 0.1 copy_bitcast_fusion
  295.4 0.8 collective-permute-done.3
  296.2 0.1 add_convert_fusion
  296.3 0.7 pad_maximum_fusion.2
  297.1 0.0 all-gather.4.cloned.1.call-update
  297.1 0.0 all-gather.6.cloned.1.call-start
  297.1 0.7 all-gather.6.cloned.1.call-update
  297.8 0.0 reduce-scatter.5.cloned.1.call-start
  297.9 0.1 copy.41
  298.0 0.1 copy.40
  298.1 78.0 %all-gather.4.cloned.1.call-done = bf16[2560,320]{1,0:T(8,128)(2,1)} async-done(((bf16[160,320]{1,0:T(8,128)(2,1)}), bf16[2560,320]{1,0:T(8,128)(2,1)}) %all-gather.4.cloned.1.call-update) | async-done | bytes 1638416 | tf_op jit(solution)/shard_map/all_gather | solution.py:140
  376.1 4.6 convolution_convert_fusion
  380.8 0.0 reduce-scatter.5.cloned.1.call-update
  380.8 89.3 %all-gather.6.cloned.1.call-done = bf16[2560,512]{1,0:T(8,128)(2,1)} async-done(((bf16[80,512]{1,0:T(8,128)(2,1)}), bf16[2560,512]{1,0:T(8,128)(2,1)}) %all-gather.6.cloned.1.call-update) | async-done | bytes 2621456 | tf_op jit(solution)/shard_map/all_gather | solution.py:143
  470.1 2.8 convolution_bitcast_fusion.2
  472.9 1.0 copy.42
  473.9 0.7 fusion.32
  474.6 120.0 %reduce-scatter.5.cloned.1.call-done = bf16[80,512]{1,0:T(8,128)(2,1)} async-done(((bf16[2560,512]{1,0:T(8,128)(2,1)}), bf16[80,512]{1,0:T(8,128)(2,1)}) %reduce-scatter.5.cloned.1.call-update) | async-done | bytes 81936 | tf_op jit(solution)/shard_map/reduce_scatter | solution.py:145
  (44 shorter events, 0.2 us)
Async XLA Ops:
  7.2 93.0 %copy-start = (bf16[160,256]{1,0:T(8,128)(2,1)S(1)}, bf16[160,256]{1,0:T(8,128)(2,1)}, u32[]{:S(2)}) copy-start(bf16[160,256]{1,0:T(8,128)(2,1)} %param.17) | copy-start | bytes 245764
  7.2 62.8 %copy-start.15 = (s32[160]{0:T(256)S(1)}, s32[160]{0:T(256)}, u32[]{:S(2)}) copy-start(s32[160]{0:T(256)} %param.19) | copy-start | bytes 1924
  7.2 62.8 %copy-start.14 = (s32[160]{0:T(256)S(1)}, s32[160]{0:T(256)}, u32[]{:S(2)}) copy-start(s32[160]{0:T(256)} %param.18) | copy-start | bytes 1924
  7.2 92.9 %copy-start.10 = (bf16[160,256]{1,0:T(8,128)(2,1)S(1)}, bf16[160,256]{1,0:T(8,128)(2,1)}, u32[]{:S(2)}) copy-start(bf16[160,256]{1,0:T(8,128)(2,1)} %param.14) | copy-start | bytes 245764
  7.2 262.0 %reduce-scatter.3.cloned.1.call-start = ((), (), s32[]{:S(2)}) async-start(), calls=%async_computation.2 | async-start | bytes 1392640 | tf_op jit(solution)/shard_map/reduce_scatter | solution.py:118
  60.7 39.5 %collective-permute-start = (bf16[2560,2,32]{0,2,1:T(8,128)(2,1)S(1)}, bf16[2560,2,32]{0,2,1:T(8,128)(2,1)S(1)}, u32[]{:S(2)}, u32[]{:S(2)}) collective-permute-start(bf16[2560,2,32]{0,2,1:T(8,128)(2,1)S(1)} %copy.31), channel_id=1, source_target_pairs={{0,1},{1,0},{2,3},{3,2},{4,5},{5,4},{6,7},{7,6},{8,9},{9,8},{10,11... | collective-permute-start | bytes 983048 | tf_op jit(solution)/shard_map/ppermute | solution.py:18
  105.4 64.4 %collective-permute-start.1 = (bf16[2560,2,64]{0,2,1:T(8,128)(2,1)S(1)}, bf16[2560,2,64]{0,2,1:T(8,128)(2,1)}, u32[]{:S(2)}, u32[]{:S(2)}) collective-permute-start(bf16[2560,2,64]{0,2,1:T(8,128)(2,1)S(1)} %copy.34), channel_id=1, source_target_pairs={{0,2},{1,3},{2,0},{3,1},{4,6},{5,7},{6,4},{7,5},{8,10},{9,11},{10,... | collective-permute-start | bytes 1966088 | tf_op jit(solution)/shard_map/ppermute | solution.py:18
  115.6 57.2 %copy-start.8 = (pred[160,2560]{1,0:T(8,128)(4,1)}, pred[160,2560]{1,0:T(8,128)(4,1)S(1)}, u32[]{:S(2)}) copy-start(pred[160,2560]{1,0:T(8,128)(4,1)S(1)} %compare_and_fusion) | copy-start | bytes 1228804
  172.9 2.2 copy-start.5
  173.1 1.1 copy-start.4
  175.1 2.7 copy-start.1
  177.9 3.1 copy-start.6
  183.4 3.3 copy-start.2
  183.4 4.0 copy-start.3
  183.4 4.0 copy-start.9
  183.4 4.0 copy-start.11
  190.3 185.9 %all-gather.4.cloned.1.call-start = ((), (), s32[]{:S(2)}) async-start(), calls=%async_computation.3 | async-start | bytes 2088960 | tf_op jit(solution)/shard_map/all_gather | solution.py:140
  190.5 2.5 copy-start.7
  193.6 104.3 %copy-start.12 = (bf16[512,32]{0,1:T(8,128)(2,1)S(1)}, bf16[512,32]{0,1:T(8,128)(2,1)}, u32[]{:S(2)}) copy-start(bf16[512,32]{0,1:T(8,128)(2,1)} %param.13) | copy-start | bytes 98308
  193.6 104.4 %copy-start.13 = (bf16[512,32]{0,1:T(8,128)(2,1)S(1)}, bf16[512,32]{0,1:T(8,128)(2,1)}, u32[]{:S(2)}) copy-start(bf16[512,32]{0,1:T(8,128)(2,1)} %param.12) | copy-start | bytes 98308
  193.6 182.5 %copy-start.17 = (bf16[512,256]{1,0:T(8,128)(2,1)S(1)}, bf16[512,256]{1,0:T(8,128)(2,1)}, u32[]{:S(2)}) copy-start(bf16[512,256]{1,0:T(8,128)(2,1)} %param.11) | copy-start | bytes 786436
  271.4 9.2 %collective-permute-start.2 = (bf16[160,2,64]{2,0,1:T(8,128)(2,1)S(1)}, bf16[160,2,64]{2,0,1:T(8,128)(2,1)S(1)}, u32[]{:S(2)}, u32[]{:S(2)}) collective-permute-start(bf16[160,2,64]{2,0,1:T(8,128)(2,1)S(1)} %select_convert_fusion.1), channel_id=1, source_target_pairs={{0,2},{1,3},{2,0},{3,1},{4,6},{5,7},{6,4},{7,5},{8,10},{9,11},{10,... | collective-permute-start | bytes 122888 | tf_op jit(solution)/shard_map/ppermute | solution.py:18
  280.9 15.3 %collective-permute-start.3 = (bf16[160,2,32]{2,0,1:T(8,128)(2,1)S(1)}, bf16[160,2,32]{2,0,1:T(8,128)(2,1)S(1)}, u32[]{:S(2)}, u32[]{:S(2)}) collective-permute-start(bf16[160,2,32]{2,0,1:T(8,128)(2,1)S(1)} %select_convert_fusion), channel_id=1, source_target_pairs={{0,1},{1,0},{2,3},{3,2},{4,5},{5,4},{6,7},{7,6},{8,9},{9,8},{10,11... | collective-permute-start | bytes 61448 | tf_op jit(solution)/shard_map/ppermute | solution.py:18
  297.1 173.0 %all-gather.6.cloned.1.call-start = ((), (), s32[]{:S(2)}) async-start(), calls=%async_computation.5 | async-start | bytes 2703360 | tf_op jit(solution)/shard_map/all_gather | solution.py:143
  297.8 296.7 %reduce-scatter.5.cloned.1.call-start = ((), (), s32[]{:S(2)}) async-start(), calls=%async_computation.4 | async-start | bytes 2703360 | tf_op jit(solution)/shard_map/reduce_scatter | solution.py:145
  380.8 89.3 %copy-start.16 = (bf16[2560,320]{1,0:T(8,128)(2,1)S(1)}, bf16[2560,320]{1,0:T(8,128)(2,1)}, u32[]{:S(2)}) copy-start(bf16[2560,320]{1,0:T(8,128)(2,1)} %all-gather.4.cloned.1.call-done) | copy-start | bytes 4915204
Sparse Core Ops, SparseCore 0:
  190.4 78.7 reduce-scatter.2
  297.2 78.8 all-gather.3
  379.3 90.7 all-gather.5
  475.0 119.5 reduce-scatter.4
where the time goes:
time: 603 us; the launch traced here: 601 us
  waiting for transfers between devices  420 us (70%)
  blocking collectives  82 us (14%)
  starting transfers between devices  41.2 us (7%)
  other arithmetic  17.9 us (3%)
  matrix products  16 us (3%)
  between operations  14.3 us (2%)
  local copies, waits for them, and re-layouts  9.56 us (2%)
    reduce_scatter x1, waiting for transfers between devices, shards(): lax.psum_scatter(contract(matching, weights_all, 1, 1).astype(jnp.bfloat1...  120 us
    all_gather x1, waiting for transfers between devices, shards(): lax.all_gather(layer_input, 'col', axis=0, tiled=True)  89.3 us
    all_gather x1, waiting for transfers between devices, shards(): grads_full = lax.all_gather(local_grads, 'row', axis=0, tiled=True)  78 us
    reduce_scatter x1, waiting for transfers between devices, shards(): lax.psum_scatter(jnp.stack([dkey_part, dvalue_part], axis=1).astype(jnp.b...  75.5 us
    ppermute x4, waiting for transfers between devices, partner_2(): return lax.ppermute(value, axis, pairs)  56.6 us
    all_gather x1, blocking collectives, shards(): key_pair = lax.all_gather(key_pair, 'row', axis=0, tiled=True)  52 us
    ppermute x4, starting transfers between devices, partner_2(): return lax.ppermute(value, axis, pairs)  40.9 us
    all_gather x1, blocking collectives, shards(): lax.all_gather(jnp.stack([positions, segment_ids]), 'row', axis=1, tiled=...  30 us
  transfers between devices with their start and end apart: 8, of which 7 were waited for; matrix products, arithmetic and copies ran while one was open for 2% of the time, Pallas kernels for 0%

commit v1 on v0

v1 whole, which is shorter than its diff:
```python
import math

import jax
import jax.numpy as jnp
from jax import lax
from jax.experimental import pallas as pl
from jax.experimental.pallas import tpu as pltpu
from jax.sharding import PartitionSpec as P

MESH = pl.DeviceIdType.MESH
BF = jnp.bfloat16
F32 = jnp.float32
HEAD = 128
TOK = 160
HALF = 80
LANES = 384
ROPE_BASE = 500000.0
SCALE = HEAD ** (-0.5)


def dot(a, b):
    return lax.dot_general(a, b, (((1,), (0,)), ((), ())), preferred_element_type=F32)


def dot_first(a, b):
    return lax.dot_general(a, b, (((0,), (0,)), ((), ())), preferred_element_type=F32)


def unrotate(first, second, cosine, sine):
    return first * cosine + second * sine, second * cosine - first * sine


def kernel(
    x_ref, wq_ref, wk_ref, wv_ref, q_ref, k_ref, v_ref, o_ref, seg_ref, cos_ref, sin_ref,
    gi_ref, gwq_ref, gwk_ref, gwv_ref,
    kv, kf, vf, sc, dw, qt, ot, qr, orow, wqt, wqtp, wkv, wkvp, wka, wkb, dqacc,
    dkp, dkr, t1, xr, t2, zr, cb, pg, pgp, dqg, dqp, xg, gi, gyr, gys, gzr, accq, acck,
    kz_s, kz_r, kx_s, kx_r, kc_s, kc_r, w_s, w_r,
    xz_s, xz_r, xy_s, xy_r, xc_s, xc_r,
    dc_s, dc_r, dx_s, dx_r, dz_s, dz_r, cx_s, cx_r, pz_s, pz_r, px_s, px_r, pc_s, pc_r,
    qz_s, qz_r, qx_s, qx_r, qc_s, qc_r, gy_s, gy_r, gz_s, gz_r,
):
    row, col = lax.axis_index("row"), lax.axis_index("col")
    x, zl = lax.div(row, 4), lax.rem(row, 4)
    y, zh, k = lax.div(col, 8), lax.rem(lax.div(col, 2), 4), lax.rem(col, 2)
    pair, h = lax.div(zh, 2), lax.rem(zh, 2)
    w = h * 4 + zl

    def device(x_=x, zl_=zl, y_=y, zh_=zh, k_=k):
        return (x_ * 4 + zl_, y_ * 8 + zh_ * 2 + k_)

    def at_x(d):
        return device(x_=lax.rem(x + d, 4))

    def at_y(d):
        return device(y_=lax.rem(y + d, 4))

    def at_zh(d):
        return device(zh_=lax.rem(zh + d, 4))

    def at_zl(d):
        return device(zl_=lax.rem(zl + d, 4))

    def at_run(e):
        there = lax.rem(w + e, 8)
        return device(zl_=lax.rem(there, 4), zh_=pair * 2 + lax.div(there, 4))

    mate = device(k_=1 - k)
    across = device(zh_=pair * 2 + 1 - h)
    diagonal = device(zh_=pair * 2 + 1 - h, k_=1 - k)
    far = [device(zh_=(1 - pair) * 2 + i) for i in range(2)]

    pending = []

    def send(src, dst, s_sem, r_sem, to):
        copy = pltpu.make_async_remote_copy(
            src_ref=src, dst_ref=dst, send_sem=s_sem, recv_sem=r_sem,
            device_id=to, device_id_type=MESH,
        )
        copy.start()
        pending.append(copy)

    def receive(dst, r_sem, s_sem):
        pltpu.make_async_remote_copy(
            src_ref=dst, dst_ref=dst, send_sem=s_sem, recv_sem=r_sem,
            device_id=mate, device_id_type=MESH,
        ).wait_recv()

    barrier = pltpu.get_barrier_semaphore()
    peers = [mate, diagonal] + far
    peers += [at_x(d) for d in (1, 2, 3)] + [at_y(d) for d in (1, 2, 3)]
    peers += [at_run(e) for e in range(1, 8)]
    for peer in peers:
        pl.semaphore_signal(barrier, inc=1, device_id=peer, device_id_type=MESH)

    keys, values = k_ref[...], v_ref[...]
    kv[k, x, w, 0:HALF, :] = jnp.concatenate(
        [keys[:HALF], values[:HALF], keys[HALF:], values[HALF:]], axis=1
    )
    first_count = jnp.sum(jnp.where(seg_ref[...] == 0, 1.0, 0.0), axis=1, keepdims=True)
    kv[k, x, w, HALF:96, :] = jnp.broadcast_to(first_count, (16, 128)).astype(BF)

    pl.semaphore_wait(barrier, len(peers))

    for e in range(1, 8):
        block = kv.at[k, x, w]
        send(block, block, kz_s.at[e], kz_r.at[e], at_run(e))

    xg[y, zh, k] = x_ref[...]
    qr[0:TOK] = q_ref[:, 0:128]
    qr[TOK : 2 * TOK] = q_ref[:, 128:256]
    qr[2 * TOK : LANES] = jnp.zeros((LANES - 2 * TOK, 128), BF)
    orow[0:TOK] = o_ref[:, 0:128]
    orow[TOK : 2 * TOK] = o_ref[:, 128:256]
    orow[2 * TOK : LANES] = jnp.zeros((LANES - 2 * TOK, 128), BF)
    qt[...] = qr[...].astype(F32).T.astype(BF)
    ot[...] = orow[...].astype(F32).T.astype(BF)
    wqt[...] = wq_ref[...].astype(F32).T.astype(BF)
    kv_weights = jnp.concatenate([wk_ref[...], wv_ref[...]], axis=1)
    wkv[...] = jnp.concatenate([kv_weights, kv_weights], axis=1).astype(F32).T.astype(BF)
    send(wqt, wqtp, w_s.at[0], w_r.at[0], mate)
    send(wkv, wkvp, w_s.at[1], w_r.at[1], mate)

    for e in range(1, 8):
        block = kv.at[k, x, lax.rem(w + 8 - e, 8)]
        receive(block, kz_r.at[e], kz_s.at[e])
    for d in (1, 3, 2):
        send(kv.at[k, x], kv.at[k, x], kx_s.at[d], kx_r.at[d], at_x(d))
    send(kv.at[k, x], kv.at[k, x], kc_s.at[0], kc_r.at[0], mate)
    for d in (1, 3, 2):
        block = xg.at[y, zh, k]
        send(block, block, xz_s.at[d], xz_r.at[d], at_zh(d))

    def products(there):
        def step(i, _):
            at = there * 4 + i
            for half in range(2):
                parts = [kv[kk, there, hh * 4 + i, 0:HALF, :] for hh in range(2) for kk in range(2)]
                lo = 64 * half
                kf[at, half * HALF : (half + 1) * HALF, :] = jnp.concatenate(
                    [p[:, lo : lo + 32] for p in parts], axis=1
                )
                vf[at, half * HALF : (half + 1) * HALF, :] = jnp.concatenate(
                    [p[:, lo + 32 : lo + 64] for p in parts], axis=1
                )
            sc[at] = dot(kf[at], qt[...]) * SCALE
            dw[at] = dot(vf[at], ot[...])
            return 0

        lax.fori_loop(0, 4, step, 0)

    receive(kv.at[1 - k, x], kc_r.at[0], kc_s.at[0])
    products(x)
    for d in (1, 3, 2):
        there = lax.rem(x + 4 - d, 4)
        receive(kv.at[k, there], kx_r.at[d], kx_s.at[d])
        send(kv.at[k, there], kv.at[k, there], kc_s.at[d], kc_r.at[d], mate)
    for d in (1, 3, 2):
        there = lax.rem(x + 4 - d, 4)
        receive(kv.at[1 - k, there], kc_r.at[d], kc_s.at[d])
        products(there)

    for d in (1, 3, 2):
        receive(xg.at[y, lax.rem(zh + 4 - d, 4), k], xz_r.at[d], xz_s.at[d])
    for d in (1, 3, 2):
        block = xg.at[y, :, k]
        send(block, block, xy_s.at[d], xy_r.at[d], at_y(d))
    block = xg.at[y, :, k]
    send(block, block, xc_s.at[0], xc_r.at[0], mate)

    cut = jnp.zeros((1, 1), F32)
    for xx in range(4):
        for zz in range(4):
            cut = cut + kv[k, xx, zz, HALF : HALF + 16, :].astype(F32)[0:1, 0:1]
    lane = lax.broadcasted_iota(jnp.int32, (1, LANES), 1)
    query = lane - TOK * (lane >= TOK).astype(jnp.int32) - TOK * (lane >= 2 * TOK).astype(jnp.int32)
    query = query + row * TOK
    cut = jnp.broadcast_to(cut, (1, LANES)).astype(jnp.int32)
    begin = jnp.where(query < cut, 0, cut)

    def mask_step(b, peak):
        key = b * TOK + lax.broadcasted_iota(jnp.int32, (TOK, LANES), 0)
        seen = jnp.where((key >= begin) & (key <= query), sc[b], -1e30)
        sc[b] = seen
        return jnp.maximum(peak, jnp.max(seen, axis=0, keepdims=True))

    peak = lax.fori_loop(0, 16, mask_step, jnp.full((1, LANES), -1e30, F32))

    def sum_step(b, sums):
        total, delta = sums
        term = jnp.exp(sc[b] - peak)
        sc[b] = term
        return (
            total + jnp.sum(term, axis=0, keepdims=True),
            delta + jnp.sum(term * dw[b], axis=0, keepdims=True),
        )

    zero = jnp.zeros((1, LANES), F32)
    total, delta = lax.fori_loop(0, 16, sum_step, (zero, zero))
    inverse = 1.0 / total
    delta = delta * inverse

    dqacc[...] = jnp.zeros_like(dqacc)
    for d in range(4):
        there = lax.rem(x + d, 4)

        def grad_step(i, _):
            b = there * 4 + i
            weights = sc[b] * inverse
            dscores = (weights * (dw[b] - delta) * SCALE).astype(BF)
            dkey = dot(dscores, qr[...]).astype(BF)
            dvalue = dot(weights.astype(BF), orow[...]).astype(BF)
            dqacc[...] += dot_first(kf[b], dscores)
            for half in range(2):
                dkp[half, there, i, 0] = dkey[half * HALF : (half + 1) * HALF]
                dkp[half, there, i, 1] = dvalue[half * HALF : (half + 1) * HALF]
            return 0

        lax.fori_loop(0, 4, grad_step, 0)
        send(dkp.at[1 - k, there], dkr.at[there], dc_s.at[d], dc_r.at[d], mate)

    cosine, sine = cos_ref[...], sin_ref[...]
    dquery = dqacc[...].T
    for head in range(2):
        part = dquery[head * TOK : (head + 1) * TOK]
        first, second = unrotate(part[:, :64], part[:, 64:], cosine, sine)
        both = jnp.concatenate([first, second], axis=1).astype(BF)
        for half in range(2):
            dqg[x, zl, half, :, head * 128 : (head + 1) * 128] = both[half * HALF : (half + 1) * HALF]
    for d in (1, 3, 2):
        block = dqg.at[x, zl]
        send(block, block, qz_s.at[d], qz_r.at[d], at_zl(d))

    for d in (1, 3, 2, 0):
        there = lax.rem(x + d, 4)
        receive(dkr.at[there], dc_r.at[d], dc_s.at[d])
        t1[there] = (dkp[k, there].astype(F32) + dkr[there].astype(F32)).astype(BF)
        if d:
            send(t1.at[there], xr.at[d], dx_s.at[d], dx_r.at[d], at_x(d))
    for d in (1, 3, 2):
        receive(xr.at[d], dx_r.at[d], dx_s.at[d])
    t2[...] = (
        t1[x].astype(F32) + xr[1].astype(F32) + xr[2].astype(F32) + xr[3].astype(F32)
    ).astype(BF)
    for e in range(1, 8):
        to = lax.rem(w + e, 8)
        send(
            t2.at[lax.rem(to, 4), lax.div(to, 4)], zr.at[e], dz_s.at[e], dz_r.at[e], at_run(e)
        )

    for d in (1, 3, 2):
        receive(dqg.at[x, lax.rem(zl + 4 - d, 4)], qz_r.at[d], qz_s.at[d])
    for d in (1, 3, 2):
        send(dqg.at[x], dqg.at[x], qx_s.at[d], qx_r.at[d], at_x(d))
    send(dqg.at[x, :, 1 - k], dqp.at[x], qc_s.at[0], qc_r.at[0], mate)

    for d in (1, 3, 2):
        there = lax.rem(y + 4 - d, 4)
        block = xg.at[there, :, k]
        receive(block, xy_r.at[d], xy_s.at[d])
        send(block, block, xc_s.at[d], xc_r.at[d], mate)

    for e in range(1, 8):
        receive(zr.at[e], dz_r.at[e], dz_s.at[e])
    summed = t2[zl, h].astype(F32)
    for e in range(1, 8):
        summed = summed + zr[e].astype(F32)
    here = pl.multiple_of(k * HALF, HALF)
    cosine, sine = cos_ref[pl.ds(here, HALF), :], sin_ref[pl.ds(here, HALF), :]
    first, second = unrotate(summed[:, :64], summed[:, 64:], cosine, sine)
    turned = jnp.concatenate([first, second], axis=1)
    cb[h, k] = jnp.where(h == 0, turned, summed).astype(BF)
    block = cb.at[h, k]
    send(block, block, cx_s.at[0], cx_r.at[0], mate)
    send(block, block, cx_s.at[1], cx_r.at[1], across)
    send(block, block, cx_s.at[2], cx_r.at[2], diagonal)
    receive(cb.at[h, 1 - k], cx_r.at[0], cx_s.at[0])
    receive(cb.at[1 - h, k], cx_r.at[1], cx_s.at[1])
    receive(cb.at[1 - h, 1 - k], cx_r.at[2], cx_s.at[2])
    source = lax.broadcasted_iota(jnp.int32, (128, 128), 0)
    target = lax.broadcasted_iota(jnp.int32, (128, 128), 1)
    wanted = (h * 2 + k) * 32 + lax.rem(target, 32)
    packed = jnp.zeros((HALF, 128), F32)
    for half in range(2):
        for which in range(2):
            group = half * 2 + which
            pick = jnp.where((source == wanted) & (lax.div(target, 32) == group), 1.0, 0.0).astype(BF)
            packed = packed + dot(cb[which, half], pick)
    pg[x, zl] = packed.astype(BF)
    for d in (1, 3, 2):
        block = pg.at[x, zl]
        send(block, block, pz_s.at[d], pz_r.at[d], at_zl(d))
    for d in (1, 3, 2):
        receive(pg.at[x, lax.rem(zl + 4 - d, 4)], pz_r.at[d], pz_s.at[d])
    for d in (1, 3, 2):
        send(pg.at[x], pg.at[x], px_s.at[d], px_r.at[d], at_x(d))
    send(pg.at[x], pgp.at[x], pc_s.at[0], pc_r.at[0], mate)

    for d in (1, 3, 2):
        there = lax.rem(x + 4 - d, 4)
        receive(dqg.at[there], qx_r.at[d], qx_s.at[d])
        send(dqg.at[there, :, 1 - k], dqp.at[there], qc_s.at[d], qc_r.at[d], mate)
    for d in (1, 3, 2):
        there = lax.rem(x + 4 - d, 4)
        receive(pg.at[there], px_r.at[d], px_s.at[d])
        send(pg.at[there], pgp.at[there], pc_s.at[d], pc_r.at[d], mate)
    receive(wqtp, w_r.at[0], w_s.at[0])
    receive(wkvp, w_r.at[1], w_s.at[1])
    for d in (0, 1, 3, 2):
        there = lax.rem(x + 4 - d, 4)
        receive(dqp.at[there], qc_r.at[d], qc_s.at[d])
        receive(pgp.at[there], pc_r.at[d], pc_s.at[d])

    mine = lax.div(lax.broadcasted_iota(jnp.int32, (128, 512), 0), 64) == k
    own_kv = jnp.where(mine, wkv[...].astype(F32), 0.0).astype(BF)
    mate_kv = jnp.where(mine, wkvp[...].astype(F32), 0.0).astype(BF)
    wka[...] = own_kv
    wkb[...] = mate_kv
    for d in (1, 3, 2, 0):
        there = lax.rem(y + d, 4)

        def input_step(i, _):
            part = (
                dot(dqg[there, i, k], wqt[...])
                + dot(dqp[there, i], wqtp[...])
                + dot(pg[there, i], wka[...])
                + dot(pgp[there, i], wkb[...])
            )
            gi[there, i] = part.astype(BF)
            return 0

        lax.fori_loop(0, 4, input_step, 0)
        if d:
            send(gi.at[there], gyr.at[d], gy_s.at[d], gy_r.at[d], at_y(d))

    for d in (0, 1, 3, 2):
        there = lax.rem(y + 4 - d, 4)
        receive(xg.at[there, :, 1 - k], xc_r.at[d], xc_s.at[d])
    accq[...] = jnp.zeros_like(accq)
    acck[...] = jnp.zeros_like(acck)

    def weight_step(i, _):
        b0, b1 = lax.div(i, 4), lax.rem(i, 4)
        accq[...] += dot_first(
            xg[b0, b1].reshape(TOK, 512), dqg[b0, b1].reshape(TOK, 256)
        )
        for half in range(2):
            acck[half] += dot_first(xg[b0, b1, half], pg[b0, b1])
        return 0

    def weight_part(first, last):
        lax.fori_loop(first, last, weight_step, 0)

    weight_part(0, 8)
    for d in (1, 3, 2):
        receive(gyr.at[d], gy_r.at[d], gy_s.at[d])

    def y_sum(i, _):
        gys[i] = (
            gi[y, i].astype(F32)
            + gyr[1, i].astype(F32)
            + gyr[2, i].astype(F32)
            + gyr[3, i].astype(F32)
        ).astype(BF)
        return 0

    lax.fori_loop(0, 4, y_sum, 0)
    for d in (1, 3, 2):
        send(gys.at[lax.rem(zh + d, 4)], gzr.at[d], gz_s.at[d], gz_r.at[d], at_zh(d))
    weight_part(8, 16)
    gwq_ref[...] = accq[...]
    gwk_ref[...] = acck[0][:, 0:32] + acck[1][:, 64:96]
    gwv_ref[...] = acck[0][:, 32:64] + acck[1][:, 96:128]
    for d in (1, 3, 2):
        receive(gzr.at[d], gz_r.at[d], gz_s.at[d])
    gi_ref[...] = (
        gys[zh].astype(F32) + gzr[1].astype(F32) + gzr[2].astype(F32) + gzr[3].astype(F32)
    ).astype(BF)
    for copy in pending:
        copy.wait_send()


def shards(
    layer_input, w_query, w_key, w_value, query, key, value, context_gradient, positions, segments
):
    half_width = HEAD // 2
    freq = jnp.exp(
        -(2.0 * jnp.arange(half_width, dtype=F32) / HEAD) * math.log(ROPE_BASE)
    )
    angle = positions.astype(F32)[:, None] * freq[None, :]
    vmem = pl.BlockSpec(memory_space=pltpu.VMEM)
    b = lambda *shape: pltpu.VMEM(shape, BF)
    f = lambda *shape: pltpu.VMEM(shape, F32)
    scratch = [
        b(2, 4, 8, 96, 128), b(16, TOK, 128), b(16, TOK, 128),
        f(16, TOK, LANES), f(16, TOK, LANES),
        b(128, LANES), b(128, LANES), b(LANES, 128), b(LANES, 128),
        b(256, 512), b(256, 512), b(128, 512), b(128, 512), b(128, 512), b(128, 512), f(128, LANES),
        b(2, 4, 4, 2, HALF, 128), b(4, 4, 2, HALF, 128), b(4, 4, 2, HALF, 128),
        b(4, 4, 2, HALF, 128), b(4, 2, HALF, 128), b(8, HALF, 128), b(2, 2, HALF, 128),
        b(4, 4, HALF, 128), b(4, 4, HALF, 128),
        b(4, 4, 2, HALF, 256), b(4, 4, HALF, 256), b(4, 4, 2, HALF, 512),
        b(4, 4, HALF, 512), b(4, 4, HALF, 512), b(4, HALF, 512), b(4, HALF, 512),
        f(512, 256), f(2, 512, 128),
    ]
    sizes = [8, 4, 4, 2, 4, 4, 4, 4, 4, 8, 3, 4, 4, 4, 4, 4, 4, 4, 4]
    for size in sizes:
        scratch += [pltpu.SemaphoreType.DMA((size,)), pltpu.SemaphoreType.DMA((size,))]
    return pl.pallas_call(
        kernel,
        out_shape=(
            jax.ShapeDtypeStruct((HALF, 512), BF),
            jax.ShapeDtypeStruct((512, 256), F32),
            jax.ShapeDtypeStruct((512, 32), F32),
            jax.ShapeDtypeStruct((512, 32), F32),
        ),
        in_specs=[vmem] * 11,
        out_specs=(vmem,) * 4,
        scratch_shapes=scratch,
        compiler_params=pltpu.CompilerParams(
            collective_id=0, has_side_effects=True, vmem_limit_bytes=48 * 2**20
        ),
        name="attention_backward",
    )(
        layer_input, w_query, w_key, w_value, query, key, value, context_gradient,
        segments.reshape(1, TOK), jnp.cos(angle), jnp.sin(angle),
    )


def solution(mesh):
    return jax.shard_map(
        shards,
        mesh=mesh,
        in_specs=(P("col", "row"),) + (P("row", "col"),) * 7 + (P("row"),) * 2,
        out_specs=(P("col", "row"), P("row", "col"), P("row", "col"), P("row", "col")),
        check_vma=False,
    )
```

time: 603 us -> 132 us (0.22)
  the two profiles are of different devices: /device:TPU:1 before, /device:TPU:46 now
where the time goes in v1:
time: 132 us
  Pallas kernels  125 us (95%)
  local copies, waits for them, and re-layouts  5.95 us (5%)
    pallas_call x1, Pallas kernels, shards(): pl.pallas_call(kernel, out_shape=(jax.ShapeDtypeStruct((HALF, 512), BF),...  125 us
    unnamed x24, local copies, waits for them, and re-layouts  4.47 us

profile of v1, /device:TPU:46, one launch (start us, length us, event | category | flops | bytes accessed | tf_op | source)
XLA Modules:
  0.0 131.6 jit_solution(4369054801576908794)
XLA Ops:
  0.6 0.0 copy-start.8
  0.7 0.7 copy-done.8
  1.3 0.0 copy-start.7
  1.3 0.0 copy-start.5
  1.3 0.8 copy.16.k_ref
  2.2 0.0 copy-done.7
  2.2 0.0 copy-start.6
  2.2 0.0 copy-start.3
  2.2 0.1 copy.17.v_ref
  2.3 0.0 copy-done.5
  2.3 0.0 copy-start
  2.3 0.1 copy.14.wk_ref
  2.4 0.5 copy-done.6
  2.9 0.1 copy.15.wv_ref
  3.1 0.0 copy-start.1
  3.1 0.0 copy-start.2
  3.1 0.4 multiply_sine_fusion
  3.4 0.0 copy-start.4
  3.5 0.0 copy-done.3
  3.5 0.0 copy-done
  3.5 0.5 copy-done.1
  4.0 0.0 copy-done.2
  4.0 0.1 copy-done.4
  4.1 124.5 %attention_backward.1 = (bf16[80,512]{1,0:T(8,128)(2,1)S(1)}, f32[512,256]{1,0:T(8,128)S(1)}, f32[512,32]{1,0:T(8,128)S(1)}, f32[512,32]{1,0:T(8,128)S(1)}) custom-call(bf16[80,512]{1,0:T(8,128)(2,1)S(1)} %copy-done.1, bf16[512,256]{1,0:T(8,128)(2,1)S(1)} %copy-done, bf16[512,32]{1,0:T(8,128)(2,1)S(1)} %copy.14.wk_ref, bf16[512,32]{1,0:T(8,128)(2,1)S(1)} %copy.15.wv_ref, ...), custom_call_target="tpu_custom_call" | custom-call | tf_op jit(solution)/shard_map/attention_backward/pallas_call | solution.py:409
  128.7 0.7 copy.18
  129.4 0.7 copy.19
  130.2 0.6 copy.22
  130.8 0.8 copy.23
  (2 shorter events, 0.0 us)
Async XLA Ops:
  0.6 0.7 copy-start.8
  1.3 0.8 copy-start.7
  1.3 1.0 copy-start.5
  2.2 0.8 copy-start.6
  2.2 1.3 copy-start.3
  2.3 1.2 copy-start
  3.1 0.9 copy-start.1
  3.1 0.9 copy-start.2
  3.4 0.7 copy-start.4

commit v2 on v1

v2 whole, which is shorter than its diff:
```python
import math

import jax
import jax.numpy as jnp
from jax import lax
from jax.experimental import pallas as pl
from jax.experimental.pallas import tpu as pltpu
from jax.sharding import PartitionSpec as P

MESH = pl.DeviceIdType.MESH
BF = jnp.bfloat16
F32 = jnp.float32
HEAD = 128
TOK = 160
HALF = 80
LANES = 384
ROPE_BASE = 500000.0
SCALE = HEAD ** (-0.5)
RUN = (4, 5, 3, 6, 2, 7, 1)


def dot(a, b):
    return lax.dot_general(a, b, (((1,), (0,)), ((), ())), preferred_element_type=F32)


def dot_first(a, b):
    return lax.dot_general(a, b, (((0,), (0,)), ((), ())), preferred_element_type=F32)


def unrotate(first, second, cosine, sine):
    return first * cosine + second * sine, second * cosine - first * sine


def kernel(
    x_ref, wq_ref, wk_ref, wv_ref, q_ref, k_ref, v_ref, o_ref, pos_ref, seg_ref,
    gi_ref, gwq_ref, gwk_ref, gwv_ref,
    kv, meta, cosine, sine, perm, kf, vf, sc, dw, ds, qt, ot, qr, orow, wqt, wqtp, wkv, wkvp, wka, wkb, dqacc,
    dkp, dkr, t1, xr, t2, zr, cb, pg, pgp, dqg, dqp, xg, gi, gyr, gys, gzr, accq, acck,
    mz_s, mz_r, mx_s, mx_r, kz_s, kz_r, kx_s, kx_r, kc_s, kc_r, w_s, w_r,
    xz_s, xz_r, xy_s, xy_r, xc_s, xc_r,
    dc_s, dc_r, dx_s, dx_r, dz_s, dz_r, cx_s, cx_r, pz_s, pz_r, px_s, px_r, pc_s, pc_r,
    qz_s, qz_r, qx_s, qx_r, qc_s, qc_r, gy_s, gy_r, gz_s, gz_r,
):
    row, col = lax.axis_index("row"), lax.axis_index("col")
    x, zl = lax.div(row, 4), lax.rem(row, 4)
    y, zh, k = lax.div(col, 8), lax.rem(lax.div(col, 2), 4), lax.rem(col, 2)
    pair, h = lax.div(zh, 2), lax.rem(zh, 2)
    w = h * 4 + zl

    def device(x_=x, zl_=zl, y_=y, zh_=zh, k_=k):
        return (x_ * 4 + zl_, y_ * 8 + zh_ * 2 + k_)

    def at_x(d):
        return device(x_=lax.rem(x + d, 4))

    def at_y(d):
        return device(y_=lax.rem(y + d, 4))

    def at_zh(d):
        return device(zh_=lax.rem(zh + d, 4))

    def at_zl(d):
        return device(zl_=lax.rem(zl + d, 4))

    def at_run(e):
        there = lax.rem(w + e, 8)
        return device(zl_=lax.rem(there, 4), zh_=pair * 2 + lax.div(there, 4))

    mate = device(k_=1 - k)
    across = device(zh_=pair * 2 + 1 - h)
    far = [device(zh_=(1 - pair) * 2 + i) for i in range(2)]

    pending = []

    def send(src, dst, s_sem, r_sem, to):
        copy = pltpu.make_async_remote_copy(
            src_ref=src, dst_ref=dst, send_sem=s_sem, recv_sem=r_sem,
            device_id=to, device_id_type=MESH,
        )
        copy.start()
        pending.append(copy)

    def receive(dst, r_sem, s_sem):
        pltpu.make_async_remote_copy(
            src_ref=dst, dst_ref=dst, send_sem=s_sem, recv_sem=r_sem,
            device_id=mate, device_id_type=MESH,
        ).wait_recv()

    barrier = pltpu.get_barrier_semaphore()
    peers = [mate] + far
    peers += [at_x(d) for d in (1, 2, 3)] + [at_y(d) for d in (1, 2, 3)]
    peers += [at_run(e) for e in range(1, 8)]
    for peer in peers:
        pl.semaphore_signal(barrier, inc=1, device_id=peer, device_id_type=MESH)

    both = jnp.concatenate([k_ref[...], v_ref[...]], axis=0).astype(F32).T
    kv[k, x, w] = jnp.concatenate([both[:HALF], both[HALF:]], axis=1).astype(BF)
    first_count = jnp.sum(jnp.where(seg_ref[...] == 0, 1.0, 0.0), axis=1, keepdims=True)
    high = lax.div(pos_ref[...], 64)
    low = pos_ref[...] - high * 64
    line = lax.broadcasted_iota(jnp.int32, (16, TOK), 0)
    facts = jnp.where(line == 0, first_count, jnp.where(line == 1, high.astype(F32), low.astype(F32)))
    meta[x, zl, :, 0:TOK] = facts.astype(BF)
    meta[x, zl, :, TOK:256] = jnp.zeros((16, 256 - TOK), BF)
    xg[y, zh, k] = x_ref[...]

    pl.semaphore_wait(barrier, len(peers))

    block = kv.at[k, x, w]
    for d in (2, 1, 3):
        send(block, block, kz_s.at[d], kz_r.at[d], at_zl(d))
    send(block, block, kz_s.at[4], kz_r.at[4], across)
    block = meta.at[x, zl]
    for d in (2, 1, 3):
        send(block, block, mz_s.at[d], mz_r.at[d], at_zl(d))
    block = kv.at[k, x, w]
    for d in (2, 1, 3):
        send(block, block, kx_s.at[d * 8], kx_r.at[d * 8], at_x(d))

    kv_weights = jnp.concatenate([wk_ref[...], wv_ref[...]], axis=0)
    wkv[...] = jnp.concatenate([kv_weights, kv_weights], axis=0)
    wqt[...] = wq_ref[...].astype(F32).T.astype(BF)
    send(wqt, wqtp, w_s.at[0], w_r.at[0], mate)
    send(wkv, wkvp, w_s.at[1], w_r.at[1], mate)
    for i in range(2):
        qr[i * TOK : (i + 1) * TOK] = q_ref[:, i * 128 : (i + 1) * 128]
        orow[i * TOK : (i + 1) * TOK] = o_ref[:, i * 128 : (i + 1) * 128]
    qr[2 * TOK : LANES] = jnp.zeros((LANES - 2 * TOK, 128), BF)
    orow[2 * TOK : LANES] = jnp.zeros((LANES - 2 * TOK, 128), BF)
    qt[...] = qr[...].astype(F32).T.astype(BF)
    ot[...] = orow[...].astype(F32).T.astype(BF)
    source = lax.broadcasted_iota(jnp.int32, (256, 256), 0)
    target = lax.broadcasted_iota(jnp.int32, (256, 256), 1)
    wanted = lax.rem(lax.div(target, 32), 2) * 128 + lax.div(target, 64) * 32 + lax.rem(target, 32)
    perm[...] = jnp.where(source == wanted, 1.0, 0.0).astype(BF)

    def run_block(e):
        if e < 4:
            return kv.at[k, x, h * 4 + lax.rem(zl + 4 - e, 4)]
        return kv.at[k, x, (1 - h) * 4 + lax.rem(zl + 8 - e, 4)]

    for e in (1, 3, 2, 4):
        block = run_block(e)
        receive(block, kz_r.at[e], kz_s.at[e])
        if e == 4:
            for d in (2, 1, 3):
                send(block, block, kz_s.at[4 + d], kz_r.at[4 + d], at_zl(d))
        for d in (2, 1, 3):
            send(block, block, kx_s.at[d * 8 + e], kx_r.at[d * 8 + e], at_x(d))
    for d in (1, 3, 2):
        receive(meta.at[x, lax.rem(zl + 4 - d, 4)], mz_r.at[d], mz_s.at[d])
    for d in (1, 3, 2):
        send(meta.at[x], meta.at[x], mx_s.at[d], mx_r.at[d], at_x(d))
    place = lax.broadcasted_iota(jnp.int32, (64, TOK), 0).astype(F32)
    freq = jnp.exp(-(2.0 * place / HEAD) * math.log(ROPE_BASE))

    def tables(i, _):
        facts = meta[x, i].astype(F32)
        angle = (facts[1:2, 0:TOK] * 64.0 + facts[2:3, 0:TOK]) * freq
        cosine[i] = jnp.cos(angle).T
        sine[i] = jnp.sin(angle).T
        return 0

    lax.fori_loop(0, 4, tables, 0)
    for e in (5, 7, 6):
        block = run_block(e)
        receive(block, kz_r.at[e], kz_s.at[e])
        for d in (2, 1, 3):
            send(block, block, kx_s.at[d * 8 + e], kx_r.at[d * 8 + e], at_x(d))
    send(kv.at[k, x], kv.at[k, x], kc_s.at[0], kc_r.at[0], mate)
    block = xg.at[y, zh, k]
    for d in (2, 1, 3):
        send(block, block, xz_s.at[d], xz_r.at[d], at_zh(d))

    for d in (1, 3, 2):
        receive(meta.at[lax.rem(x + 4 - d, 4)], mx_r.at[d], mx_s.at[d])
    cut = jnp.zeros((1, 1), F32)
    for xx in range(4):
        for zz in range(4):
            cut = cut + meta[xx, zz].astype(F32)[0:1, 0:1]
    lane = lax.broadcasted_iota(jnp.int32, (1, LANES), 1)
    query = lane - TOK * (lane >= TOK).astype(jnp.int32) - TOK * (lane >= 2 * TOK).astype(jnp.int32)
    query = query + row * TOK
    cut = jnp.broadcast_to(cut, (1, LANES)).astype(jnp.int32)
    begin = jnp.where(query < cut, 0, cut)

    def products(there, peak):
        def step(i, peak):
            at = there * 4 + i
            for half in range(2):
                parts = [kv[kk, there, hh * 4 + i] for hh in range(2) for kk in range(2)]
                lo = 64 * half
                kf[at, half * HALF : (half + 1) * HALF, :] = jnp.concatenate(
                    [p[:, lo : lo + 32] for p in parts], axis=1
                )
                vf[at, half * HALF : (half + 1) * HALF, :] = jnp.concatenate(
                    [p[:, lo + 32 : lo + 64] for p in parts], axis=1
                )
            dw[at] = dot(vf[at], ot[...])
            key = at * TOK + lax.broadcasted_iota(jnp.int32, (TOK, LANES), 0)
            seen = (key >= begin) & (key <= query)
            seen = jnp.where(seen, dot(kf[at], qt[...]) * SCALE, -1e30)
            sc[at] = seen
            return jnp.maximum(peak, jnp.max(seen, axis=0, keepdims=True))

        return lax.fori_loop(0, 4, step, peak)

    receive(kv.at[1 - k, x], kc_r.at[0], kc_s.at[0])
    peak = products(x, jnp.full((1, LANES), -1e30, F32))
    for d in (1, 3, 2):
        there = lax.rem(x + 4 - d, 4)
        for e in range(8):
            at = h * 4 + lax.rem(zl + 4 - e, 4) if e < 4 else (1 - h) * 4 + lax.rem(zl + 8 - e, 4)
            block = kv.at[k, there, at]
            receive(block, kx_r.at[d * 8 + e], kx_s.at[d * 8 + e])
        send(kv.at[k, there], kv.at[k, there], kc_s.at[d], kc_r.at[d], mate)
    for d in (1, 3, 2):
        there = lax.rem(x + 4 - d, 4)
        receive(kv.at[1 - k, there], kc_r.at[d], kc_s.at[d])
        peak = products(there, peak)


    def sum_step(b, sums):
        total, delta = sums
        term = jnp.exp(sc[b] - peak)
        sc[b] = term
        return (
            total + jnp.sum(term, axis=0, keepdims=True),
            delta + jnp.sum(term * dw[b], axis=0, keepdims=True),
        )

    zero = jnp.zeros((1, LANES), F32)
    total, delta = lax.fori_loop(0, 16, sum_step, (zero, zero))
    inverse = 1.0 / total
    delta = delta * inverse

    dqacc[...] = jnp.zeros_like(dqacc)
    cosines, sines = cosine[zl], sine[zl]

    def key_sum(d):
        there = lax.rem(x + d, 4)
        receive(dkr.at[there], dc_r.at[d], dc_s.at[d])
        t1[there] = (dkp[k, there].astype(F32) + dkr[there].astype(F32)).astype(BF)
        if d:
            send(t1.at[there], xr.at[d], dx_s.at[d], dx_r.at[d], at_x(d))

    before = None
    for d in (2, 1, 3, 0):
        there = lax.rem(x + d, 4)

        def grad_step(i, _):
            b = there * 4 + i
            weights = sc[b] * inverse
            dscores = (weights * (dw[b] - delta) * SCALE).astype(BF)
            ds[i] = dscores
            dkey = dot(dscores, qr[...]).astype(BF)
            dvalue = dot(weights.astype(BF), orow[...]).astype(BF)
            for half in range(2):
                dkp[half, there, i, 0] = dkey[half * HALF : (half + 1) * HALF]
                dkp[half, there, i, 1] = dvalue[half * HALF : (half + 1) * HALF]
            return 0

        lax.fori_loop(0, 4, grad_step, 0)
        send(dkp.at[1 - k, there], dkr.at[there], dc_s.at[d], dc_r.at[d], mate)
        dqacc[...] += dot_first(
            kf[pl.ds(there * 4, 4)].reshape(4 * TOK, HEAD), ds[...].reshape(4 * TOK, LANES)
        )
        if before is not None:
            key_sum(before)
        before = d

    dquery = dqacc[...].T
    for head in range(2):
        part = dquery[head * TOK : (head + 1) * TOK]
        first, second = unrotate(part[:, :64], part[:, 64:], cosines, sines)
        both = jnp.concatenate([first, second], axis=1).astype(BF)
        for half in range(2):
            dqg[x, zl, half, :, head * 128 : (head + 1) * 128] = both[half * HALF : (half + 1) * HALF]
    block = dqg.at[x, zl]
    for d in (1, 3, 2):
        send(block, block, qz_s.at[d], qz_r.at[d], at_zl(d))
    key_sum(0)
    for d in (1, 3, 2):
        receive(xg.at[y, lax.rem(zh + 4 - d, 4), k], xz_r.at[d], xz_s.at[d])
    block = xg.at[y, :, k]
    for d in (2, 1, 3):
        send(block, block, xy_s.at[d], xy_r.at[d], at_y(d))
    send(block, block, xc_s.at[0], xc_r.at[0], mate)
    for d in (1, 3, 2):
        receive(xr.at[d], dx_r.at[d], dx_s.at[d])
    here = pl.multiple_of(k * HALF, HALF)

    def x_sum(i, _):
        total = t1[x, i].astype(F32)
        for d in range(1, 4):
            total = total + xr[d, i].astype(F32)
        first, second = unrotate(
            total[0, :, :64], total[0, :, 64:],
            cosine[i, pl.ds(here, HALF), :], sine[i, pl.ds(here, HALF), :],
        )
        wide = jnp.concatenate([first, second, total[1]], axis=1).astype(BF)
        wide = dot(wide, perm[...]).astype(BF)
        t2[i, 0] = wide[:, :128]
        t2[i, 1] = wide[:, 128:]
        return 0

    lax.fori_loop(0, 4, x_sum, 0)
    for e in RUN:
        to = lax.rem(w + e, 8)
        send(
            t2.at[lax.rem(to, 4), lax.div(to, 4)], zr.at[e], dz_s.at[e], dz_r.at[e], at_run(e)
        )

    for d in (1, 3, 2):
        receive(dqg.at[x, lax.rem(zl + 4 - d, 4)], qz_r.at[d], qz_s.at[d])
    for d in (2, 1, 3):
        send(dqg.at[x], dqg.at[x], qx_s.at[d], qx_r.at[d], at_x(d))
    send(dqg.at[x, :, 1 - k], dqp.at[x], qc_s.at[0], qc_r.at[0], mate)

    for d in (1, 3, 2):
        there = lax.rem(y + 4 - d, 4)
        block = xg.at[there, :, k]
        receive(block, xy_r.at[d], xy_s.at[d])
        send(block, block, xc_s.at[d], xc_r.at[d], mate)

    for e in range(1, 8):
        receive(zr.at[e], dz_r.at[e], dz_s.at[e])
    summed = t2[zl, h].astype(F32)
    for e in range(1, 8):
        summed = summed + zr[e].astype(F32)
    cb[k] = summed.astype(BF)
    send(cb.at[k], cb.at[k], cx_s.at[0], cx_r.at[0], mate)
    receive(cb.at[1 - k], cx_r.at[0], cx_s.at[0])
    halves = [
        jnp.concatenate([cb[0][:, lo : lo + 64], cb[1][:, lo : lo + 64]], axis=1) for lo in (0, 64)
    ]
    pg[x, zl] = jnp.where(k == 0, halves[0].astype(F32), halves[1].astype(F32)).astype(BF)
    for d in (1, 3, 2):
        block = pg.at[x, zl]
        send(block, block, pz_s.at[d], pz_r.at[d], at_zl(d))
    for d in (1, 3, 2):
        receive(pg.at[x, lax.rem(zl + 4 - d, 4)], pz_r.at[d], pz_s.at[d])
    for d in (1, 3, 2):
        send(pg.at[x], pg.at[x], px_s.at[d], px_r.at[d], at_x(d))
    send(pg.at[x], pgp.at[x], pc_s.at[0], pc_r.at[0], mate)

    for d in (1, 3, 2):
        there = lax.rem(x + 4 - d, 4)
        receive(dqg.at[there], qx_r.at[d], qx_s.at[d])
        send(dqg.at[there, :, 1 - k], dqp.at[there], qc_s.at[d], qc_r.at[d], mate)
    for d in (1, 3, 2):
        there = lax.rem(x + 4 - d, 4)
        receive(pg.at[there], px_r.at[d], px_s.at[d])
        send(pg.at[there], pgp.at[there], pc_s.at[d], pc_r.at[d], mate)
    receive(wqtp, w_r.at[0], w_s.at[0])
    receive(wkvp, w_r.at[1], w_s.at[1])
    for d in (0, 1, 3, 2):
        there = lax.rem(x + 4 - d, 4)
        receive(dqp.at[there], qc_r.at[d], qc_s.at[d])
        receive(pgp.at[there], pc_r.at[d], pc_s.at[d])

    mine = lax.div(lax.broadcasted_iota(jnp.int32, (128, 512), 0), 64) == k
    own_kv = jnp.where(mine, wkv[...].astype(F32), 0.0).astype(BF)
    mate_kv = jnp.where(mine, wkvp[...].astype(F32), 0.0).astype(BF)
    wka[...] = own_kv
    wkb[...] = mate_kv
    def input_part(c):
        part = slice(c * 128, (c + 1) * 128)

        def input_step(there, _):
            gi[c, there] = (
                (
                    dot(dqg[there, :, k].reshape(4 * HALF, 256), wqt[:, part])
                    + dot(dqp[there].reshape(4 * HALF, 256), wqtp[:, part])
                    + dot(pg[there].reshape(4 * HALF, 128), wka[:, part])
                    + dot(pgp[there].reshape(4 * HALF, 128), wkb[:, part])
                )
                .astype(BF)
                .reshape(4, HALF, 128)
            )
            return 0

        lax.fori_loop(0, 4, input_step, 0)

    def input_send(c):
        for d in (2, 1, 3):
            send(
                gi.at[c, lax.rem(y + d, 4)], gyr.at[c, d],
                gy_s.at[c * 4 + d], gy_r.at[c * 4 + d], at_y(d),
            )

    for c in range(4):
        input_part(c)
        if c < 2:
            input_send(c)

    for d in (0, 1, 3, 2):
        there = lax.rem(y + 4 - d, 4)
        receive(xg.at[there, :, 1 - k], xc_r.at[d], xc_s.at[d])
    accq[...] = jnp.zeros_like(accq)
    acck[...] = jnp.zeros_like(acck)

    def weight_step(i, _):
        b0, b1 = lax.div(i, 4), lax.rem(i, 4)
        accq[...] += dot_first(xg[b0, b1].reshape(TOK, 512), dqg[b0, b1].reshape(TOK, 256))
        for half in range(2):
            acck[half] += dot_first(pg[b0, b1], xg[b0, b1, half])
        return 0

    def weight_part(first, last):
        lax.fori_loop(first, last, weight_step, 0)

    weight_part(0, 4)
    for c in range(4):
        for d in (1, 3, 2):
            receive(gyr.at[c, d], gy_r.at[c * 4 + d], gy_s.at[c * 4 + d])
        if c < 2:
            input_send(c + 2)
        gys[c] = (
            gi[c, y].astype(F32)
            + gyr[c, 1].astype(F32)
            + gyr[c, 2].astype(F32)
            + gyr[c, 3].astype(F32)
        ).astype(BF)
        for d in (2, 1, 3):
            send(
                gys.at[c, lax.rem(zh + d, 4)], gzr.at[c, d],
                gz_s.at[c * 4 + d], gz_r.at[c * 4 + d], at_zh(d),
            )
        if c < 3:
            weight_part(4 + c * 3, 7 + c * 3)
    weight_part(13, 16)
    gwq_ref[...] = accq[...]
    gwk_ref[...] = acck[0, 0:32] + acck[1, 64:96]
    gwv_ref[...] = acck[0, 32:64] + acck[1, 96:128]
    for c in range(4):
        for d in (1, 3, 2):
            receive(gzr.at[c, d], gz_r.at[c * 4 + d], gz_s.at[c * 4 + d])
        gi_ref[:, c * 128 : (c + 1) * 128] = (
            gys[c, zh].astype(F32)
            + gzr[c, 1].astype(F32)
            + gzr[c, 2].astype(F32)
            + gzr[c, 3].astype(F32)
        ).astype(BF)
    for copy in pending:
        copy.wait_send()


def shards(
    layer_input, w_query, w_key, w_value, query, key, value, context_gradient, positions, segments
):
    vmem = pl.BlockSpec(memory_space=pltpu.VMEM)
    b = lambda *shape: pltpu.VMEM(shape, BF)
    f = lambda *shape: pltpu.VMEM(shape, F32)
    scratch = [
        b(2, 4, 8, HALF, 128), b(4, 4, 16, 256), f(4, TOK, 64), f(4, TOK, 64), b(256, 256),
        b(16, TOK, 128), b(16, TOK, 128), f(16, TOK, LANES), f(16, TOK, LANES), b(4, TOK, LANES),
        b(128, LANES), b(128, LANES), b(LANES, 128), b(LANES, 128),
        b(256, 512), b(256, 512), b(128, 512), b(128, 512), b(128, 512), b(128, 512), f(128, LANES),
        b(2, 4, 4, 2, HALF, 128), b(4, 4, 2, HALF, 128), b(4, 4, 2, HALF, 128),
        b(4, 4, 2, HALF, 128), b(4, 2, HALF, 128), b(8, HALF, 128), b(2, HALF, 128),
        b(4, 4, HALF, 128), b(4, 4, HALF, 128),
        b(4, 4, 2, HALF, 256), b(4, 4, HALF, 256), b(4, 4, 2, HALF, 512),
        b(4, 4, 4, HALF, 128), b(4, 4, 4, HALF, 128), b(4, 4, HALF, 128), b(4, 4, HALF, 128),
        f(512, 256), f(2, 128, 512),
    ]
    sizes = [4, 4, 8, 32, 4, 2, 4, 4, 4, 4, 4, 8, 1, 4, 4, 4, 4, 4, 4, 16, 16]
    for size in sizes:
        scratch += [pltpu.SemaphoreType.DMA((size,)), pltpu.SemaphoreType.DMA((size,))]
    gi, gwq, gwk, gwv = pl.pallas_call(
        kernel,
        out_shape=(
            jax.ShapeDtypeStruct((HALF, 512), BF),
            jax.ShapeDtypeStruct((512, 256), F32),
            jax.ShapeDtypeStruct((32, 512), F32),
            jax.ShapeDtypeStruct((32, 512), F32),
        ),
        in_specs=[vmem] * 10,
        out_specs=(vmem,) * 4,
        scratch_shapes=scratch,
        compiler_params=pltpu.CompilerParams(
            collective_id=0, has_side_effects=True, vmem_limit_bytes=48 * 2**20
        ),
        name="attention_backward",
    )(
        layer_input, w_query, w_key.T, w_value.T, query, key.T, value.T, context_gradient,
        positions.reshape(1, TOK), segments.reshape(1, TOK),
    )
    return gi, gwq, gwk.T, gwv.T


def solution(mesh):
    return jax.shard_map(
        shards,
        mesh=mesh,
        in_specs=(P("col", "row"),) + (P("row", "col"),) * 7 + (P("row"),) * 2,
        out_specs=(P("col", "row"), P("row", "col"), P("row", "col"), P("row", "col")),
        check_vma=False,
    )
```

time: 132 us -> 116 us (0.88)
  the two profiles are of different devices: /device:TPU:46 before, /device:TPU:1 now
where the time goes in v2:
time: 116 us
  Pallas kernels  105 us (91%)
  local copies, waits for them, and re-layouts  9.92 us (9%)
    pallas_call x1, Pallas kernels, shards(): pl.pallas_call(kernel, out_shape=(jax.ShapeDtypeStruct((HALF, 512), BF),...  105 us
    unnamed x24, local copies, waits for them, and re-layouts  9.92 us

profile of v2, /device:TPU:1, one launch (start us, length us, event | category | flops | bytes accessed | tf_op | source)
XLA Modules:
  0.0 115.7 jit_solution(13849357034012718672)
XLA Ops:
  0.6 0.0 copy-start.9
  0.6 0.0 copy-start.8
  0.7 0.7 copy-done.9
  1.3 0.0 copy-done.8
  1.3 0.0 copy-start
  1.3 0.9 copy-done
  2.3 0.0 copy-start.1
  2.3 0.9 copy-done.1
  3.2 0.0 copy-start.2
  3.2 0.9 copy-done.2
  4.1 0.0 copy-start.3
  4.1 0.9 copy-done.3
  4.9 0.0 copy-start.4
  4.9 0.8 copy-done.4
  5.7 0.0 copy-start.5
  5.7 0.8 copy-done.5
  6.5 0.0 copy-start.6
  6.5 0.7 copy-done.6
  7.2 0.0 copy-start.7
  7.2 0.7 copy-done.7
  7.9 105.1 %attention_backward.1 = (bf16[80,512]{1,0:T(8,128)(2,1)S(1)}, f32[512,256]{1,0:T(8,128)S(1)}, f32[32,512]{1,0:T(8,128)S(1)}, f32[32,512]{1,0:T(8,128)S(1)}) custom-call(bf16[80,512]{1,0:T(8,128)(2,1)S(1)} %copy-done.1, bf16[512,256]{1,0:T(8,128)(2,1)S(1)} %copy-done, bf16[32,512]{1,0:T(8,128)(2,1)S(1)} %bitcast.10, bf16[32,512]{1,0:T(8,128)(2,1)S(1)} %bitcast.11, ...), custom_call_target="tpu_custom_call" | custom-call | tf_op jit(solution)/shard_map/attention_backward/pallas_call | solution.py:470
  113.0 0.6 copy.18
  113.6 0.8 copy.19
  114.4 0.6 copy.20
  115.0 0.6 copy.21
Async XLA Ops:
  0.6 0.7 copy-start.9
  0.6 0.7 copy-start.8
  1.3 0.9 copy-start
  2.3 0.9 copy-start.1
  3.2 0.9 copy-start.2
  4.1 0.9 copy-start.3
  4.9 0.8 copy-start.4
  5.7 0.8 copy-start.5
  6.5 0.7 copy-start.6
  7.2 0.7 copy-start.7

commit v3 on v2

--- a/solution.py
+++ b/solution.py
@@ -15,8 +15,10 @@
 HALF = 80
 LANES = 384
 ROPE_BASE = 500000.0
+VMEM_BYTES = 127 * 2**19
 SCALE = HEAD ** (-0.5)
 RUN = (4, 5, 3, 6, 2, 7, 1)
+ROWS = (pl.ds(0, 48), pl.ds(48, 32))
 
 
 def dot(a, b):
@@ -32,14 +34,15 @@
 
 
 def kernel(
-    x_ref, wq_ref, wk_ref, wv_ref, q_ref, k_ref, v_ref, o_ref, pos_ref, seg_ref,
+    x_hbm, wq_hbm, wk_hbm, wv_hbm, q_hbm, k_hbm, v_hbm, o_hbm, pos_hbm, seg_hbm,
     gi_ref, gwq_ref, gwk_ref, gwv_ref,
-    kv, meta, cosine, sine, perm, kf, vf, sc, dw, ds, qt, ot, qr, orow, wqt, wqtp, wkv, wkvp, wka, wkb, dqacc,
-    dkp, dkr, t1, xr, t2, zr, cb, pg, pgp, dqg, dqp, xg, gi, gyr, gys, gzr, accq, acck,
-    mz_s, mz_r, mx_s, mx_r, kz_s, kz_r, kx_s, kx_r, kc_s, kc_r, w_s, w_r,
+    wq_ref, wk_ref, wv_ref, q_ref, k_ref, v_ref, o_ref, pos_ref, seg_ref,
+    kv, meta, cosine, sine, perm, kf, vf, sc, dw, ds, qt, ot, qr, orow, wqt, wkv, dqacc,
+    dkp, dkr, t1, xr, t2, zr, gk, gkm, dqo, dqg, dqm, xg, gi, gyr, gys, gzr, accq, acck,
+    load, mz_s, mz_r, mx_s, mx_r, kz_s, kz_r, kx_s, kx_r, kc_s, kc_r, w_s, w_r,
     xz_s, xz_r, xy_s, xy_r, xc_s, xc_r,
-    dc_s, dc_r, dx_s, dx_r, dz_s, dz_r, cx_s, cx_r, pz_s, pz_r, px_s, px_r, pc_s, pc_r,
-    qz_s, qz_r, qx_s, qx_r, qc_s, qc_r, gy_s, gy_r, gz_s, gz_r,
+    dc_s, dc_r, dx_s, dx_r, dz_s, dz_r, pz_s, pz_r, px_s, px_r, pc_s, pc_r,
+    qm_s, qm_r, qz_s, qz_r, qx_s, qx_r, qc_s, qc_r, gy_s, gy_r, gz_s, gz_r,
 ):
     row, col = lax.axis_index("row"), lax.axis_index("col")
     x, zl = lax.div(row, 4), lax.rem(row, 4)
@@ -92,6 +95,19 @@
     peers += [at_run(e) for e in range(1, 8)]
     for peer in peers:
         pl.semaphore_signal(barrier, inc=1, device_id=peer, device_id_type=MESH)
+
+    loads = [
+        pltpu.make_async_copy(src, dst, load.at[i])
+        for i, (src, dst) in enumerate([
+            (k_hbm, k_ref), (v_hbm, v_ref), (pos_hbm, pos_ref), (seg_hbm, seg_ref),
+            (x_hbm, xg.at[y, zh, k]), (wk_hbm, wk_ref), (wv_hbm, wv_ref), (wq_hbm, wq_ref),
+            (q_hbm, q_ref), (o_hbm, o_ref),
+        ])
+    ]
+    for copy in loads:
+        copy.start()
+    for copy in loads[:4]:
+        copy.wait()
 
     both = jnp.concatenate([k_ref[...], v_ref[...]], axis=0).astype(F32).T
     kv[k, x, w] = jnp.concatenate([both[:HALF], both[HALF:]], axis=1).astype(BF)
@@ -102,7 +118,6 @@
     facts = jnp.where(line == 0, first_count, jnp.where(line == 1, high.astype(F32), low.astype(F32)))
     meta[x, zl, :, 0:TOK] = facts.astype(BF)
     meta[x, zl, :, TOK:256] = jnp.zeros((16, 256 - TOK), BF)
-    xg[y, zh, k] = x_ref[...]
 
     pl.semaphore_wait(barrier, len(peers))
 
@@ -117,11 +132,14 @@
     for d in (2, 1, 3):
         send(block, block, kx_s.at[d * 8], kx_r.at[d * 8], at_x(d))
 
-    kv_weights = jnp.concatenate([wk_ref[...], wv_ref[...]], axis=0)
-    wkv[...] = jnp.concatenate([kv_weights, kv_weights], axis=0)
-    wqt[...] = wq_ref[...].astype(F32).T.astype(BF)
-    send(wqt, wqtp, w_s.at[0], w_r.at[0], mate)
-    send(wkv, wkvp, w_s.at[1], w_r.at[1], mate)
+    for copy in loads[4:]:
+        copy.wait()
+    rows = pl.ds(pl.multiple_of(k * 64, 64), 64)
+    wkv[rows, :] = jnp.concatenate([wk_ref[...], wv_ref[...]], axis=0)
+    send(wkv.at[rows], wkv.at[rows], w_s.at[1], w_r.at[1], mate)
+    rows = pl.ds(pl.multiple_of(k * 256, 256), 256)
+    wqt[rows, :] = wq_ref[...].astype(F32).T.astype(BF)
+    send(wqt.at[rows], wqt.at[rows], w_s.at[0], w_r.at[0], mate)
     for i in range(2):
         qr[i * TOK : (i + 1) * TOK] = q_ref[:, i * 128 : (i + 1) * 128]
         orow[i * TOK : (i + 1) * TOK] = o_ref[:, i * 128 : (i + 1) * 128]
@@ -237,12 +255,19 @@
     dqacc[...] = jnp.zeros_like(dqacc)
     cosines, sines = cosine[zl], sine[zl]
 
+    def key_send(d, part):
+        there, rows = lax.rem(x + d, 4), ROWS[part]
+        send(
+            t1.at[there, :, :, rows], xr.at[d, :, :, rows],
+            dx_s.at[d * 2 + part], dx_r.at[d * 2 + part], at_x(d),
+        )
+
     def key_sum(d):
         there = lax.rem(x + d, 4)
         receive(dkr.at[there], dc_r.at[d], dc_s.at[d])
         t1[there] = (dkp[k, there].astype(F32) + dkr[there].astype(F32)).astype(BF)
         if d:
-            send(t1.at[there], xr.at[d], dx_s.at[d], dx_r.at[d], at_x(d))
+            key_send(d, 0)
 
     before = None
     for d in (2, 1, 3, 0):
@@ -275,105 +300,105 @@
         first, second = unrotate(part[:, :64], part[:, 64:], cosines, sines)
         both = jnp.concatenate([first, second], axis=1).astype(BF)
         for half in range(2):
-            dqg[x, zl, half, :, head * 128 : (head + 1) * 128] = both[half * HALF : (half + 1) * HALF]
+            dqo[half, :, head * 128 : (head + 1) * 128] = both[half * HALF : (half + 1) * HALF]
+    mine = pl.ds(pl.multiple_of(k * 256, 256), 256)
+    other = pl.ds(pl.multiple_of((1 - k) * 256, 256), 256)
+    send(dqo.at[1 - k], dqg.at[x, zl, :, mine], qm_s.at[0], qm_r.at[0], mate)
+    dqg[x, zl, :, mine] = dqo[k]
+    key_sum(0)
+    receive(dqg.at[x, zl, :, other], qm_r.at[0], qm_s.at[0])
     block = dqg.at[x, zl]
-    for d in (1, 3, 2):
+    for d in (2, 1, 3):
         send(block, block, qz_s.at[d], qz_r.at[d], at_zl(d))
-    key_sum(0)
+    for d in (2, 1, 3):
+        key_send(d, 1)
+    for d in (2, 1, 3):
+        send(block, block, qx_s.at[d * 4], qx_r.at[d * 4], at_x(d))
+
     for d in (1, 3, 2):
         receive(xg.at[y, lax.rem(zh + 4 - d, 4), k], xz_r.at[d], xz_s.at[d])
     block = xg.at[y, :, k]
     for d in (2, 1, 3):
         send(block, block, xy_s.at[d], xy_r.at[d], at_y(d))
     send(block, block, xc_s.at[0], xc_r.at[0], mate)
-    for d in (1, 3, 2):
-        receive(xr.at[d], dx_r.at[d], dx_s.at[d])
-    here = pl.multiple_of(k * HALF, HALF)
-
-    def x_sum(i, _):
-        total = t1[x, i].astype(F32)
-        for d in range(1, 4):
-            total = total + xr[d, i].astype(F32)
-        first, second = unrotate(
-            total[0, :, :64], total[0, :, 64:],
-            cosine[i, pl.ds(here, HALF), :], sine[i, pl.ds(here, HALF), :],
-        )
-        wide = jnp.concatenate([first, second, total[1]], axis=1).astype(BF)
-        wide = dot(wide, perm[...]).astype(BF)
-        t2[i, 0] = wide[:, :128]
-        t2[i, 1] = wide[:, 128:]
-        return 0
-
-    lax.fori_loop(0, 4, x_sum, 0)
-    for e in RUN:
-        to = lax.rem(w + e, 8)
-        send(
-            t2.at[lax.rem(to, 4), lax.div(to, 4)], zr.at[e], dz_s.at[e], dz_r.at[e], at_run(e)
-        )
-
-    for d in (1, 3, 2):
-        receive(dqg.at[x, lax.rem(zl + 4 - d, 4)], qz_r.at[d], qz_s.at[d])
-    for d in (2, 1, 3):
-        send(dqg.at[x], dqg.at[x], qx_s.at[d], qx_r.at[d], at_x(d))
-    send(dqg.at[x, :, 1 - k], dqp.at[x], qc_s.at[0], qc_r.at[0], mate)
-
-    for d in (1, 3, 2):
-        there = lax.rem(y + 4 - d, 4)
-        block = xg.at[there, :, k]
-        receive(block, xy_r.at[d], xy_s.at[d])
-        send(block, block, xc_s.at[d], xc_r.at[d], mate)
-
-    for e in range(1, 8):
-        receive(zr.at[e], dz_r.at[e], dz_s.at[e])
+
+    def x_sum(part):
+        lo, size = (0, 48) if part == 0 else (48, 32)
+        at = pl.ds(pl.multiple_of(k * HALF + lo, 16), size)
+
+        def step(i, _):
+            total = t1[x, i, :, lo : lo + size].astype(F32)
+            for d in range(1, 4):
+                total = total + xr[d, i, :, lo : lo + size].astype(F32)
+            first, second = unrotate(
+                total[0, :, :64], total[0, :, 64:], cosine[i, at, :], sine[i, at, :]
+            )
+            wide = jnp.concatenate([first, second, total[1]], axis=1).astype(BF)
+            wide = dot(wide, perm[...]).astype(BF)
+            t2[i, 0, lo : lo + size] = wide[:, :128]
+            t2[i, 1, lo : lo + size] = wide[:, 128:]
+            return 0
+
+        lax.fori_loop(0, 4, step, 0)
+
+    for part in range(2):
+        for d in (1, 3, 2):
+            rows = ROWS[part]
+            receive(xr.at[d, :, :, rows], dx_r.at[d * 2 + part], dx_s.at[d * 2 + part])
+        x_sum(part)
+        for e in RUN:
+            to = lax.rem(w + e, 8)
+            send(
+                t2.at[lax.rem(to, 4), lax.div(to, 4), rows], zr.at[e, rows],
+                dz_s.at[e * 2 + part], dz_r.at[e * 2 + part], at_run(e),
+            )
+
+    for e in (1, 3, 2):
+        block = dqg.at[x, lax.rem(zl + 4 - e, 4)]
+        receive(block, qz_r.at[e], qz_s.at[e])
+        for d in (2, 1, 3):
+            send(block, block, qx_s.at[d * 4 + e], qx_r.at[d * 4 + e], at_x(d))
+
+    for part in range(2):
+        for e in RUN:
+            rows = ROWS[part]
+            receive(zr.at[e, rows], dz_r.at[e * 2 + part], dz_s.at[e * 2 + part])
     summed = t2[zl, h].astype(F32)
     for e in range(1, 8):
         summed = summed + zr[e].astype(F32)
-    cb[k] = summed.astype(BF)
-    send(cb.at[k], cb.at[k], cx_s.at[0], cx_r.at[0], mate)
-    receive(cb.at[1 - k], cx_r.at[0], cx_s.at[0])
-    halves = [
-        jnp.concatenate([cb[0][:, lo : lo + 64], cb[1][:, lo : lo + 64]], axis=1) for lo in (0, 64)
-    ]
-    pg[x, zl] = jnp.where(k == 0, halves[0].astype(F32), halves[1].astype(F32)).astype(BF)
-    for d in (1, 3, 2):
-        block = pg.at[x, zl]
+    gk[x, zl] = summed.astype(BF)
+    block = gk.at[x, zl]
+    for d in (2, 1, 3):
         send(block, block, pz_s.at[d], pz_r.at[d], at_zl(d))
-    for d in (1, 3, 2):
-        receive(pg.at[x, lax.rem(zl + 4 - d, 4)], pz_r.at[d], pz_s.at[d])
-    for d in (1, 3, 2):
-        send(pg.at[x], pg.at[x], px_s.at[d], px_r.at[d], at_x(d))
-    send(pg.at[x], pgp.at[x], pc_s.at[0], pc_r.at[0], mate)
-
+    for d in (2, 1, 3):
+        send(block, block, px_s.at[d * 4], px_r.at[d * 4], at_x(d))
+    for e in (1, 3, 2):
+        block = gk.at[x, lax.rem(zl + 4 - e, 4)]
+        receive(block, pz_r.at[e], pz_s.at[e])
+        for d in (2, 1, 3):
+            send(block, block, px_s.at[d * 4 + e], px_r.at[d * 4 + e], at_x(d))
+
+    receive(wqt.at[pl.ds(pl.multiple_of((1 - k) * 256, 256), 256)], w_r.at[0], w_s.at[0])
+    receive(wkv.at[pl.ds(pl.multiple_of((1 - k) * 64, 64), 64)], w_r.at[1], w_s.at[1])
     for d in (1, 3, 2):
         there = lax.rem(x + 4 - d, 4)
-        receive(dqg.at[there], qx_r.at[d], qx_s.at[d])
-        send(dqg.at[there, :, 1 - k], dqp.at[there], qc_s.at[d], qc_r.at[d], mate)
+        for e in range(4):
+            block = dqg.at[there, lax.rem(zl + 4 - e, 4)]
+            receive(block, qx_r.at[d * 4 + e], qx_s.at[d * 4 + e])
     for d in (1, 3, 2):
         there = lax.rem(x + 4 - d, 4)
-        receive(pg.at[there], px_r.at[d], px_s.at[d])
-        send(pg.at[there], pgp.at[there], pc_s.at[d], pc_r.at[d], mate)
-    receive(wqtp, w_r.at[0], w_s.at[0])
-    receive(wkvp, w_r.at[1], w_s.at[1])
-    for d in (0, 1, 3, 2):
-        there = lax.rem(x + 4 - d, 4)
-        receive(dqp.at[there], qc_r.at[d], qc_s.at[d])
-        receive(pgp.at[there], pc_r.at[d], pc_s.at[d])
-
-    mine = lax.div(lax.broadcasted_iota(jnp.int32, (128, 512), 0), 64) == k
-    own_kv = jnp.where(mine, wkv[...].astype(F32), 0.0).astype(BF)
-    mate_kv = jnp.where(mine, wkvp[...].astype(F32), 0.0).astype(BF)
-    wka[...] = own_kv
-    wkb[...] = mate_kv
+        for e in range(4):
+            block = gk.at[there, lax.rem(zl + 4 - e, 4)]
+            receive(block, px_r.at[d * 4 + e], px_s.at[d * 4 + e])
+
     def input_part(c):
         part = slice(c * 128, (c + 1) * 128)
 
         def input_step(there, _):
             gi[c, there] = (
                 (
-                    dot(dqg[there, :, k].reshape(4 * HALF, 256), wqt[:, part])
-                    + dot(dqp[there].reshape(4 * HALF, 256), wqtp[:, part])
-                    + dot(pg[there].reshape(4 * HALF, 128), wka[:, part])
-                    + dot(pgp[there].reshape(4 * HALF, 128), wkb[:, part])
+                    dot(dqg[there].reshape(4 * HALF, 512), wqt[:, part])
+                    + dot(gk[there].reshape(4 * HALF, 128), wkv[:, part])
                 )
                 .astype(BF)
                 .reshape(4, HALF, 128)
@@ -394,23 +419,36 @@
         if c < 2:
             input_send(c)
 
+    for d in (1, 3, 2):
+        there = lax.rem(y + 4 - d, 4)
+        block = xg.at[there, :, k]
+        receive(block, xy_r.at[d], xy_s.at[d])
+        send(block, block, xc_s.at[d], xc_r.at[d], mate)
+    for there in range(4):
+        send(dqg.at[there, :, :, other], dqm.at[there], qc_s.at[there], qc_r.at[there], mate)
+        send(gk.at[there], gkm.at[there], pc_s.at[there], pc_r.at[there], mate)
+    for there in range(4):
+        receive(dqm.at[there], qc_r.at[there], qc_s.at[there])
+        receive(gkm.at[there], pc_r.at[there], pc_s.at[there])
     for d in (0, 1, 3, 2):
         there = lax.rem(y + 4 - d, 4)
         receive(xg.at[there, :, 1 - k], xc_r.at[d], xc_s.at[d])
     accq[...] = jnp.zeros_like(accq)
     acck[...] = jnp.zeros_like(acck)
 
-    def weight_step(i, _):
-        b0, b1 = lax.div(i, 4), lax.rem(i, 4)
-        accq[...] += dot_first(xg[b0, b1].reshape(TOK, 512), dqg[b0, b1].reshape(TOK, 256))
-        for half in range(2):
-            acck[half] += dot_first(pg[b0, b1], xg[b0, b1, half])
+    def weight_step(b, _):
+        here = xg[b, :, k].reshape(4 * HALF, 512)
+        accq[...] += dot_first(here, dqg[b, :, :, mine].reshape(4 * HALF, 256))
+        acck[...] += dot_first(gk[b].reshape(4 * HALF, 128), here)
+        here = xg[b, :, 1 - k].reshape(4 * HALF, 512)
+        accq[...] += dot_first(here, dqm[b].reshape(4 * HALF, 256))
+        acck[...] += dot_first(gkm[b].reshape(4 * HALF, 128), here)
         return 0
 
     def weight_part(first, last):
         lax.fori_loop(first, last, weight_step, 0)
 
-    weight_part(0, 4)
+    weight_part(0, 1)
     for c in range(4):
         for d in (1, 3, 2):
             receive(gyr.at[c, d], gy_r.at[c * 4 + d], gy_s.at[c * 4 + d])
@@ -428,11 +466,10 @@
                 gz_s.at[c * 4 + d], gz_r.at[c * 4 + d], at_zh(d),
             )
         if c < 3:
-            weight_part(4 + c * 3, 7 + c * 3)
-    weight_part(13, 16)
+            weight_part(1 + c, 2 + c)
     gwq_ref[...] = accq[...]
-    gwk_ref[...] = acck[0, 0:32] + acck[1, 64:96]
-    gwv_ref[...] = acck[0, 32:64] + acck[1, 96:128]
+    gwk_ref[...] = acck[pl.ds(pl.multiple_of(k * 64, 64), 32), :]
+    gwv_ref[...] = acck[pl.ds(pl.multiple_of(k * 64 + 32, 32), 32), :]
     for c in range(4):
         for d in (1, 3, 2):
             receive(gzr.at[c, d], gz_r.at[c * 4 + d], gz_s.at[c * 4 + d])
@@ -446,6 +483,19 @@
         copy.wait_send()
 
 
+def write_out(a, b, c, d, a_out, b_out, c_out, d_out, a_tmp, b_tmp, c_tmp, d_tmp, sems):
+    ins, temps, outs = (a, b, c, d), (a_tmp, b_tmp, c_tmp, d_tmp), (a_out, b_out, c_out, d_out)
+    reads = [pltpu.make_async_copy(ins[i], temps[i], sems.at[0, i]) for i in range(4)]
+    writes = [pltpu.make_async_copy(temps[i], outs[i], sems.at[1, i]) for i in range(4)]
+    for read in reads:
+        read.start()
+    for read, write in zip(reads, writes):
+        read.wait()
+        write.start()
+    for write in writes:
+        write.wait()
+
+
 def shards(
     layer_input, w_query, w_key, w_value, query, key, value, context_gradient, positions, segments
 ):
@@ -453,18 +503,20 @@
     b = lambda *shape: pltpu.VMEM(shape, BF)
     f = lambda *shape: pltpu.VMEM(shape, F32)
     scratch = [
+        b(512, 256), b(32, 512), b(32, 512), b(TOK, 256), b(32, TOK), b(32, TOK), b(TOK, 256),
+        pltpu.VMEM((1, TOK), jnp.int32), pltpu.VMEM((1, TOK), jnp.int32),
         b(2, 4, 8, HALF, 128), b(4, 4, 16, 256), f(4, TOK, 64), f(4, TOK, 64), b(256, 256),
         b(16, TOK, 128), b(16, TOK, 128), f(16, TOK, LANES), f(16, TOK, LANES), b(4, TOK, LANES),
         b(128, LANES), b(128, LANES), b(LANES, 128), b(LANES, 128),
-        b(256, 512), b(256, 512), b(128, 512), b(128, 512), b(128, 512), b(128, 512), f(128, LANES),
+        b(512, 512), b(128, 512), f(128, LANES),
         b(2, 4, 4, 2, HALF, 128), b(4, 4, 2, HALF, 128), b(4, 4, 2, HALF, 128),
-        b(4, 4, 2, HALF, 128), b(4, 2, HALF, 128), b(8, HALF, 128), b(2, HALF, 128),
+        b(4, 4, 2, HALF, 128), b(4, 2, HALF, 128), b(8, HALF, 128),
         b(4, 4, HALF, 128), b(4, 4, HALF, 128),
-        b(4, 4, 2, HALF, 256), b(4, 4, HALF, 256), b(4, 4, 2, HALF, 512),
+        b(2, HALF, 256), b(4, 4, HALF, 512), b(4, 4, HALF, 256), b(4, 4, 2, HALF, 512),
         b(4, 4, 4, HALF, 128), b(4, 4, 4, HALF, 128), b(4, 4, HALF, 128), b(4, 4, HALF, 128),
-        f(512, 256), f(2, 128, 512),
+        f(512, 256), f(128, 512), pltpu.SemaphoreType.DMA((10,)),
     ]
-    sizes = [4, 4, 8, 32, 4, 2, 4, 4, 4, 4, 4, 8, 1, 4, 4, 4, 4, 4, 4, 16, 16]
+    sizes = [4, 4, 8, 32, 4, 2, 4, 4, 4, 4, 8, 16, 4, 16, 4, 1, 4, 16, 4, 16, 16]
     for size in sizes:
         scratch += [pltpu.SemaphoreType.DMA((size,)), pltpu.SemaphoreType.DMA((size,))]
     gi, gwq, gwk, gwv = pl.pallas_call(
@@ -475,17 +527,29 @@
             jax.ShapeDtypeStruct((32, 512), F32),
             jax.ShapeDtypeStruct((32, 512), F32),
         ),
-        in_specs=[vmem] * 10,
+        in_specs=[pl.BlockSpec(memory_space=pl.ANY)] * 10,
         out_specs=(vmem,) * 4,
         scratch_shapes=scratch,
         compiler_params=pltpu.CompilerParams(
-            collective_id=0, has_side_effects=True, vmem_limit_bytes=48 * 2**20
+            collective_id=0, has_side_effects=True, vmem_limit_bytes=VMEM_BYTES
         ),
         name="attention_backward",
     )(
         layer_input, w_query, w_key.T, w_value.T, query, key.T, value.T, context_gradient,
         positions.reshape(1, TOK), segments.reshape(1, TOK),
     )
+    results = (gi, gwq, gwk, gwv)
+    anywhere = pl.BlockSpec(memory_space=pl.ANY)
+    gi, gwq, gwk, gwv = pl.pallas_call(
+        write_out,
+        out_shape=tuple(jax.ShapeDtypeStruct(r.shape, r.dtype) for r in results),
+        in_specs=[anywhere] * 4,
+        out_specs=(anywhere,) * 4,
+        scratch_shapes=[pltpu.VMEM(r.shape, r.dtype) for r in results]
+        + [pltpu.SemaphoreType.DMA((2, 4))],
+        compiler_params=pltpu.CompilerParams(vmem_limit_bytes=VMEM_BYTES),
+        name="write_out",
+    )(*results)
     return gi, gwq, gwk.T, gwv.T
 
 

time: 116 us -> 106 us (0.914)
  local copies, waits for them, and re-layouts: 9.92 us -> 0 us
    unnamed x24 -> x0, local copies, waits for them, and re-layouts: 9.92 us -> none
    pallas_call x0 -> x1, Pallas kernels: none -> 1.98 us  [shards(): pl.pallas_call(write_out, out_shape=tuple((jax.ShapeDtypeStruct(r.shape,...]
    pallas_call x1, Pallas kernels: 105 us -> 104 us  [shards(): pl.pallas_call(kernel, out_shape=(jax.ShapeDtypeStruct((HALF, 512), BF),...]
where the time goes in v3:
time: 106 us
  Pallas kernels  106 us (100%)
    pallas_call x1, Pallas kernels, shards(): pl.pallas_call(kernel, out_shape=(jax.ShapeDtypeStruct((HALF, 512), BF),...  104 us

profile of v3, /device:TPU:1, one launch (start us, length us, event | category | flops | bytes accessed | tf_op | source)
XLA Modules:
  0.0 106.2 jit_solution(1236262286642695694)
XLA Ops:
  0.6 103.6 %attention_backward.1 = (bf16[80,512]{1,0:T(8,128)(2,1)}, f32[512,256]{1,0:T(8,128)}, f32[32,512]{1,0:T(8,128)}, f32[32,512]{1,0:T(8,128)}) custom-call(bf16[80,512]{1,0:T(8,128)(2,1)} %x_hbm.1, bf16[512,256]{1,0:T(8,128)(2,1)} %wq_hbm.1, bf16[32,512]{1,0:T(8,128)(2,1)} %bitcast.8, bf16[32,512]{1,0:T(8,128)(2,1)} %bitcast.9, bf16[160,256]{1,0:T(8,128)(2,1)} %q_hbm.1, ...), custom_call_target="tpu_custom_call" | custom-call | tf_op jit(solution)/shard_map/attention_backward/pallas_call | solution.py:522
  104.2 2.0 %write_out.1 = (bf16[80,512]{1,0:T(8,128)(2,1)}, f32[512,256]{1,0:T(8,128)}, f32[32,512]{1,0:T(8,128)}, f32[32,512]{1,0:T(8,128)}) custom-call(bf16[80,512]{1,0:T(8,128)(2,1)} %get-tuple-element.12.a, f32[512,256]{1,0:T(8,128)} %get-tuple-element.13.b, f32[32,512]{1,0:T(8,128)} %get-tuple-element.14.c, f32[32,512]{1,0:T(8,128)} %get-tuple-element.15.d), custom_call_target="tpu_custom_call" | custom-call | tf_op jit(solution)/shard_map/write_out/pallas_call | solution.py:543

commit v4 on v3

--- a/solution.py
+++ b/solution.py
@@ -29,20 +29,20 @@
     return lax.dot_general(a, b, (((0,), (0,)), ((), ())), preferred_element_type=F32)
 
 
-def unrotate(first, second, cosine, sine):
-    return first * cosine + second * sine, second * cosine - first * sine
+def unrotate(gradient, cosines, sines):
+    return gradient * cosines + pltpu.roll(gradient, HEAD // 2, 1) * sines
 
 
 def kernel(
     x_hbm, wq_hbm, wk_hbm, wv_hbm, q_hbm, k_hbm, v_hbm, o_hbm, pos_hbm, seg_hbm,
     gi_ref, gwq_ref, gwk_ref, gwv_ref,
     wq_ref, wk_ref, wv_ref, q_ref, k_ref, v_ref, o_ref, pos_ref, seg_ref,
-    kv, meta, cosine, sine, perm, kf, vf, sc, dw, ds, qt, ot, qr, orow, wqt, wkv, dqacc,
+    kv, meta, cosine, sine, perm, kf, vf, sc, dw, ds, low, qt, ot, qr, orow, wqt, wkv, dqacc,
     dkp, dkr, t1, xr, t2, zr, gk, gkm, dqo, dqg, dqm, xg, gi, gyr, gys, gzr, accq, acck,
     load, mz_s, mz_r, mx_s, mx_r, kz_s, kz_r, kx_s, kx_r, kc_s, kc_r, w_s, w_r,
     xz_s, xz_r, xy_s, xy_r, xc_s, xc_r,
     dc_s, dc_r, dx_s, dx_r, dz_s, dz_r, pz_s, pz_r, px_s, px_r, pc_s, pc_r,
-    qm_s, qm_r, qz_s, qz_r, qx_s, qx_r, qc_s, qc_r, gy_s, gy_r, gz_s, gz_r,
+    qm_s, qm_r, qz_s, qz_r, qx_s, qx_r, q2_s, q2_r, qc_s, qc_r, gy_s, gy_r, gz_s, gz_r,
 ):
     row, col = lax.axis_index("row"), lax.axis_index("col")
     x, zl = lax.div(row, 4), lax.rem(row, 4)
@@ -82,6 +82,7 @@
         )
         copy.start()
         pending.append(copy)
+        return copy
 
     def receive(dst, r_sem, s_sem):
         pltpu.make_async_remote_copy(
@@ -113,9 +114,9 @@
     kv[k, x, w] = jnp.concatenate([both[:HALF], both[HALF:]], axis=1).astype(BF)
     first_count = jnp.sum(jnp.where(seg_ref[...] == 0, 1.0, 0.0), axis=1, keepdims=True)
     high = lax.div(pos_ref[...], 64)
-    low = pos_ref[...] - high * 64
+    rest = pos_ref[...] - high * 64
     line = lax.broadcasted_iota(jnp.int32, (16, TOK), 0)
-    facts = jnp.where(line == 0, first_count, jnp.where(line == 1, high.astype(F32), low.astype(F32)))
+    facts = jnp.where(line == 0, first_count, jnp.where(line == 1, high.astype(F32), rest.astype(F32)))
     meta[x, zl, :, 0:TOK] = facts.astype(BF)
     meta[x, zl, :, TOK:256] = jnp.zeros((16, 256 - TOK), BF)
 
@@ -129,17 +130,11 @@
     for d in (2, 1, 3):
         send(block, block, mz_s.at[d], mz_r.at[d], at_zl(d))
     block = kv.at[k, x, w]
-    for d in (2, 1, 3):
+    for d in (1, 3):
         send(block, block, kx_s.at[d * 8], kx_r.at[d * 8], at_x(d))
 
     for copy in loads[4:]:
         copy.wait()
-    rows = pl.ds(pl.multiple_of(k * 64, 64), 64)
-    wkv[rows, :] = jnp.concatenate([wk_ref[...], wv_ref[...]], axis=0)
-    send(wkv.at[rows], wkv.at[rows], w_s.at[1], w_r.at[1], mate)
-    rows = pl.ds(pl.multiple_of(k * 256, 256), 256)
-    wqt[rows, :] = wq_ref[...].astype(F32).T.astype(BF)
-    send(wqt.at[rows], wqt.at[rows], w_s.at[0], w_r.at[0], mate)
     for i in range(2):
         qr[i * TOK : (i + 1) * TOK] = q_ref[:, i * 128 : (i + 1) * 128]
         orow[i * TOK : (i + 1) * TOK] = o_ref[:, i * 128 : (i + 1) * 128]
@@ -147,10 +142,6 @@
     orow[2 * TOK : LANES] = jnp.zeros((LANES - 2 * TOK, 128), BF)
     qt[...] = qr[...].astype(F32).T.astype(BF)
     ot[...] = orow[...].astype(F32).T.astype(BF)
-    source = lax.broadcasted_iota(jnp.int32, (256, 256), 0)
-    target = lax.broadcasted_iota(jnp.int32, (256, 256), 1)
-    wanted = lax.rem(lax.div(target, 32), 2) * 128 + lax.div(target, 64) * 32 + lax.rem(target, 32)
-    perm[...] = jnp.where(source == wanted, 1.0, 0.0).astype(BF)
 
     def run_block(e):
         if e < 4:
@@ -163,33 +154,27 @@
         if e == 4:
             for d in (2, 1, 3):
                 send(block, block, kz_s.at[4 + d], kz_r.at[4 + d], at_zl(d))
-        for d in (2, 1, 3):
+        for d in (1, 3):
             send(block, block, kx_s.at[d * 8 + e], kx_r.at[d * 8 + e], at_x(d))
     for d in (1, 3, 2):
         receive(meta.at[x, lax.rem(zl + 4 - d, 4)], mz_r.at[d], mz_s.at[d])
     for d in (1, 3, 2):
         send(meta.at[x], meta.at[x], mx_s.at[d], mx_r.at[d], at_x(d))
-    place = lax.broadcasted_iota(jnp.int32, (64, TOK), 0).astype(F32)
-    freq = jnp.exp(-(2.0 * place / HEAD) * math.log(ROPE_BASE))
-
-    def tables(i, _):
-        facts = meta[x, i].astype(F32)
-        angle = (facts[1:2, 0:TOK] * 64.0 + facts[2:3, 0:TOK]) * freq
-        cosine[i] = jnp.cos(angle).T
-        sine[i] = jnp.sin(angle).T
-        return 0
-
-    lax.fori_loop(0, 4, tables, 0)
     for e in (5, 7, 6):
         block = run_block(e)
         receive(block, kz_r.at[e], kz_s.at[e])
-        for d in (2, 1, 3):
+        for d in (1, 3):
             send(block, block, kx_s.at[d * 8 + e], kx_r.at[d * 8 + e], at_x(d))
+    send(kv.at[k, x], kv.at[k, x], kx_s.at[16], kx_r.at[16], at_x(2))
     send(kv.at[k, x], kv.at[k, x], kc_s.at[0], kc_r.at[0], mate)
     block = xg.at[y, zh, k]
     for d in (2, 1, 3):
         send(block, block, xz_s.at[d], xz_r.at[d], at_zh(d))
 
+    source = lax.broadcasted_iota(jnp.int32, (256, 256), 0)
+    target = lax.broadcasted_iota(jnp.int32, (256, 256), 1)
+    wanted = lax.rem(lax.div(target, 32), 2) * 128 + lax.div(target, 64) * 32 + lax.rem(target, 32)
+    perm[...] = jnp.where(source == wanted, 1.0, 0.0).astype(BF)
     for d in (1, 3, 2):
         receive(meta.at[lax.rem(x + 4 - d, 4)], mx_r.at[d], mx_s.at[d])
     cut = jnp.zeros((1, 1), F32)
@@ -221,21 +206,41 @@
             sc[at] = seen
             return jnp.maximum(peak, jnp.max(seen, axis=0, keepdims=True))
 
-        return lax.fori_loop(0, 4, step, peak)
+        return lax.fori_loop(0, 4, step, peak, unroll=2)
 
     receive(kv.at[1 - k, x], kc_r.at[0], kc_s.at[0])
     peak = products(x, jnp.full((1, LANES), -1e30, F32))
-    for d in (1, 3, 2):
+    place = lax.broadcasted_iota(jnp.int32, (HEAD, TOK), 0)
+    freq = jnp.exp(-(2.0 * lax.rem(place, 64).astype(F32) / HEAD) * math.log(ROPE_BASE))
+    sign = jnp.where(place < 64, 1.0, -1.0)
+
+    def tables(i, _):
+        facts = meta[x, i].astype(F32)
+        angle = (facts[1:2, 0:TOK] * 64.0 + facts[2:3, 0:TOK]) * freq
+        cosine[i] = jnp.cos(angle).T
+        sine[i] = (jnp.sin(angle) * sign).T
+        return 0
+
+    lax.fori_loop(0, 4, tables, 0)
+    def pass_on(d):
         there = lax.rem(x + 4 - d, 4)
-        for e in range(8):
-            at = h * 4 + lax.rem(zl + 4 - e, 4) if e < 4 else (1 - h) * 4 + lax.rem(zl + 8 - e, 4)
-            block = kv.at[k, there, at]
-            receive(block, kx_r.at[d * 8 + e], kx_s.at[d * 8 + e])
+        if d == 2:
+            receive(kv.at[k, there], kx_r.at[16], kx_s.at[16])
+        else:
+            for e in range(8):
+                near = h * 4 + lax.rem(zl + 4 - e, 4)
+                at = near if e < 4 else (1 - h) * 4 + lax.rem(zl + 8 - e, 4)
+                receive(kv.at[k, there, at], kx_r.at[d * 8 + e], kx_s.at[d * 8 + e])
         send(kv.at[k, there], kv.at[k, there], kc_s.at[d], kc_r.at[d], mate)
+
+    pass_on(1)
+    pass_on(3)
     for d in (1, 3, 2):
         there = lax.rem(x + 4 - d, 4)
         receive(kv.at[1 - k, there], kc_r.at[d], kc_s.at[d])
         peak = products(there, peak)
+        if d == 1:
+            pass_on(2)
 
 
     def sum_step(b, sums):
@@ -269,52 +274,66 @@
         if d:
             key_send(d, 0)
 
-    before = None
-    for d in (2, 1, 3, 0):
-        there = lax.rem(x + d, 4)
-
-        def grad_step(i, _):
+    def score_grads(there, _):
+        for i in range(4):
             b = there * 4 + i
             weights = sc[b] * inverse
-            dscores = (weights * (dw[b] - delta) * SCALE).astype(BF)
-            ds[i] = dscores
-            dkey = dot(dscores, qr[...]).astype(BF)
-            dvalue = dot(weights.astype(BF), orow[...]).astype(BF)
-            for half in range(2):
-                dkp[half, there, i, 0] = dkey[half * HALF : (half + 1) * HALF]
-                dkp[half, there, i, 1] = dvalue[half * HALF : (half + 1) * HALF]
-            return 0
-
-        lax.fori_loop(0, 4, grad_step, 0)
-        send(dkp.at[1 - k, there], dkr.at[there], dc_s.at[d], dc_r.at[d], mate)
+            ds[b] = (weights * (dw[b] - delta) * SCALE).astype(BF)
+            low[b] = weights.astype(BF)
         dqacc[...] += dot_first(
-            kf[pl.ds(there * 4, 4)].reshape(4 * TOK, HEAD), ds[...].reshape(4 * TOK, LANES)
+            kf[pl.ds(there * 4, 4)].reshape(4 * TOK, HEAD),
+            ds[pl.ds(there * 4, 4)].reshape(4 * TOK, LANES),
         )
-        if before is not None:
-            key_sum(before)
-        before = d
-
+        return 0
+
+    lax.fori_loop(0, 4, score_grads, 0)
     dquery = dqacc[...].T
     for head in range(2):
         part = dquery[head * TOK : (head + 1) * TOK]
-        first, second = unrotate(part[:, :64], part[:, 64:], cosines, sines)
-        both = jnp.concatenate([first, second], axis=1).astype(BF)
+        both = unrotate(part, cosines, sines).astype(BF)
         for half in range(2):
             dqo[half, :, head * 128 : (head + 1) * 128] = both[half * HALF : (half + 1) * HALF]
     mine = pl.ds(pl.multiple_of(k * 256, 256), 256)
     other = pl.ds(pl.multiple_of((1 - k) * 256, 256), 256)
     send(dqo.at[1 - k], dqg.at[x, zl, :, mine], qm_s.at[0], qm_r.at[0], mate)
     dqg[x, zl, :, mine] = dqo[k]
+
+    before = None
+    for d in (2, 1, 3, 0):
+        there = lax.rem(x + d, 4)
+
+        def grad_step(i, _):
+            b = there * 4 + i
+            dkey = dot(ds[b], qr[...]).astype(BF)
+            dvalue = dot(low[b], orow[...]).astype(BF)
+            for half in range(2):
+                dkp[half, there, i, 0] = dkey[half * HALF : (half + 1) * HALF]
+                dkp[half, there, i, 1] = dvalue[half * HALF : (half + 1) * HALF]
+            return 0
+
+        lax.fori_loop(0, 4, grad_step, 0, unroll=2)
+        send(dkp.at[1 - k, there], dkr.at[there], dc_s.at[d], dc_r.at[d], mate)
+        if before is None:
+            receive(dqg.at[x, zl, :, other], qm_r.at[0], qm_s.at[0])
+            block = dqg.at[x, zl]
+            for e in (2, 1, 3):
+                send(block, block, qz_s.at[e], qz_r.at[e], at_zl(e))
+        else:
+            key_sum(before)
+        before = d
     key_sum(0)
-    receive(dqg.at[x, zl, :, other], qm_r.at[0], qm_s.at[0])
+    for d in (2, 1, 3):
+        key_send(d, 1)
     block = dqg.at[x, zl]
-    for d in (2, 1, 3):
-        send(block, block, qz_s.at[d], qz_r.at[d], at_zl(d))
-    for d in (2, 1, 3):
-        key_send(d, 1)
-    for d in (2, 1, 3):
+    for d in (1, 3):
         send(block, block, qx_s.at[d * 4], qx_r.at[d * 4], at_x(d))
 
+    rows = pl.ds(pl.multiple_of(k * 64, 64), 64)
+    wkv[rows, :] = jnp.concatenate([wk_ref[...], wv_ref[...]], axis=0)
+    send(wkv.at[rows], wkv.at[rows], w_s.at[1], w_r.at[1], mate)
+    rows = pl.ds(pl.multiple_of(k * 256, 256), 256)
+    wqt[rows, :] = wq_ref[...].astype(F32).T.astype(BF)
+    send(wqt.at[rows], wqt.at[rows], w_s.at[0], w_r.at[0], mate)
     for d in (1, 3, 2):
         receive(xg.at[y, lax.rem(zh + 4 - d, 4), k], xz_r.at[d], xz_s.at[d])
     block = xg.at[y, :, k]
@@ -330,16 +349,14 @@
             total = t1[x, i, :, lo : lo + size].astype(F32)
             for d in range(1, 4):
                 total = total + xr[d, i, :, lo : lo + size].astype(F32)
-            first, second = unrotate(
-                total[0, :, :64], total[0, :, 64:], cosine[i, at, :], sine[i, at, :]
-            )
-            wide = jnp.concatenate([first, second, total[1]], axis=1).astype(BF)
+            turned = unrotate(total[0], cosine[i, at, :], sine[i, at, :])
+            wide = jnp.concatenate([turned, total[1]], axis=1).astype(BF)
             wide = dot(wide, perm[...]).astype(BF)
             t2[i, 0, lo : lo + size] = wide[:, :128]
             t2[i, 1, lo : lo + size] = wide[:, 128:]
             return 0
 
-        lax.fori_loop(0, 4, step, 0)
+        lax.fori_loop(0, 4, step, 0, unroll=True)
 
     for part in range(2):
         for d in (1, 3, 2):
@@ -356,8 +373,17 @@
     for e in (1, 3, 2):
         block = dqg.at[x, lax.rem(zl + 4 - e, 4)]
         receive(block, qz_r.at[e], qz_s.at[e])
-        for d in (2, 1, 3):
+        for d in (1, 3):
             send(block, block, qx_s.at[d * 4 + e], qx_r.at[d * 4 + e], at_x(d))
+
+    def relay(e):
+        for part, d in enumerate((1, 3)):
+            block = dqg.at[lax.rem(x + 4 - d, 4), lax.rem(zl + 4 - e, 4)]
+            receive(block, qx_r.at[d * 4 + e], qx_s.at[d * 4 + e])
+            block = block.at[:, pl.ds(part * 256, 256)]
+            send(block, block, q2_s.at[part * 4 + e], q2_r.at[part * 4 + e], at_x(d))
+
+    relay(0)
 
     for part in range(2):
         for e in RUN:
@@ -373,18 +399,24 @@
     for d in (2, 1, 3):
         send(block, block, px_s.at[d * 4], px_r.at[d * 4], at_x(d))
     for e in (1, 3, 2):
+        relay(e)
+    for e in (1, 3, 2):
         block = gk.at[x, lax.rem(zl + 4 - e, 4)]
         receive(block, pz_r.at[e], pz_s.at[e])
         for d in (2, 1, 3):
             send(block, block, px_s.at[d * 4 + e], px_r.at[d * 4 + e], at_x(d))
+    for d in (1, 3, 2):
+        there = lax.rem(y + 4 - d, 4)
+        block = xg.at[there, :, k]
+        receive(block, xy_r.at[d], xy_s.at[d])
+        send(block, block, xc_s.at[d], xc_r.at[d], mate)
 
     receive(wqt.at[pl.ds(pl.multiple_of((1 - k) * 256, 256), 256)], w_r.at[0], w_s.at[0])
     receive(wkv.at[pl.ds(pl.multiple_of((1 - k) * 64, 64), 64)], w_r.at[1], w_s.at[1])
-    for d in (1, 3, 2):
-        there = lax.rem(x + 4 - d, 4)
-        for e in range(4):
-            block = dqg.at[there, lax.rem(zl + 4 - e, 4)]
-            receive(block, qx_r.at[d * 4 + e], qx_s.at[d * 4 + e])
+    for e in range(4):
+        for part in range(2):
+            block = dqg.at[lax.rem(x + 2, 4), lax.rem(zl + 4 - e, 4), :, pl.ds(part * 256, 256)]
+            receive(block, q2_r.at[part * 4 + e], q2_s.at[part * 4 + e])
     for d in (1, 3, 2):
         there = lax.rem(x + 4 - d, 4)
         for e in range(4):
@@ -392,38 +424,54 @@
             receive(block, px_r.at[d * 4 + e], px_s.at[d * 4 + e])
 
     def input_part(c):
-        part = slice(c * 128, (c + 1) * 128)
-
-        def input_step(there, _):
-            gi[c, there] = (
-                (
-                    dot(dqg[there].reshape(4 * HALF, 512), wqt[:, part])
-                    + dot(gk[there].reshape(4 * HALF, 128), wkv[:, part])
-                )
-                .astype(BF)
-                .reshape(4, HALF, 128)
+        rows = slice(c * 16, (c + 1) * 16)
+        gi[c] = (
+            (
+                dot(dqg[:, :, rows, :].reshape(256, 512), wqt[...])
+                + dot(gk[:, :, rows, :].reshape(256, 128), wkv[...])
             )
-            return 0
-
-        lax.fori_loop(0, 4, input_step, 0)
+            .astype(BF)
+            .reshape(4, 4, 16, 512)
+        )
 
     def input_send(c):
-        for d in (2, 1, 3):
+        return [
             send(
                 gi.at[c, lax.rem(y + d, 4)], gyr.at[c, d],
                 gy_s.at[c * 4 + d], gy_r.at[c * 4 + d], at_y(d),
             )
-
-    for c in range(4):
+            for d in (2, 1, 3)
+        ]
+
+    def sent(copies):
+        for copy in copies:
+            copy.wait_send()
+            pending[:] = [other for other in pending if other is not copy]
+
+    def input_sum(c):
+        for d in (1, 3, 2):
+            receive(gyr.at[c, d], gy_r.at[c * 4 + d], gy_s.at[c * 4 + d])
+        gys[c] = (
+            gi[c, y].astype(F32)
+            + gyr[c, 1].astype(F32)
+            + gyr[c, 2].astype(F32)
+            + gyr[c, 3].astype(F32)
+        ).astype(BF)
+        for d in (2, 1, 3):
+            send(
+                gys.at[c, lax.rem(zh + d, 4)], gzr.at[c, d],
+                gz_s.at[c * 4 + d], gz_r.at[c * 4 + d], at_zh(d),
+            )
+
+    flying = []
+    for c in range(5):
         input_part(c)
-        if c < 2:
-            input_send(c)
-
-    for d in (1, 3, 2):
-        there = lax.rem(y + 4 - d, 4)
-        block = xg.at[there, :, k]
-        receive(block, xy_r.at[d], xy_s.at[d])
-        send(block, block, xc_s.at[d], xc_r.at[d], mate)
+        if c == 4:
+            input_sum(0)
+        if c >= 2:
+            sent(flying[c - 2])
+        flying.append(input_send(c))
+
     for there in range(4):
         send(dqg.at[there, :, :, other], dqm.at[there], qc_s.at[there], qc_r.at[there], mate)
         send(gk.at[there], gkm.at[there], pc_s.at[there], pc_r.at[there], mate)
@@ -449,31 +497,17 @@
         lax.fori_loop(first, last, weight_step, 0)
 
     weight_part(0, 1)
-    for c in range(4):
-        for d in (1, 3, 2):
-            receive(gyr.at[c, d], gy_r.at[c * 4 + d], gy_s.at[c * 4 + d])
-        if c < 2:
-            input_send(c + 2)
-        gys[c] = (
-            gi[c, y].astype(F32)
-            + gyr[c, 1].astype(F32)
-            + gyr[c, 2].astype(F32)
-            + gyr[c, 3].astype(F32)
-        ).astype(BF)
-        for d in (2, 1, 3):
-            send(
-                gys.at[c, lax.rem(zh + d, 4)], gzr.at[c, d],
-                gz_s.at[c * 4 + d], gz_r.at[c * 4 + d], at_zh(d),
-            )
-        if c < 3:
-            weight_part(1 + c, 2 + c)
+    for c in range(1, 5):
+        input_sum(c)
+        if c < 4:
+            weight_part(c, c + 1)
     gwq_ref[...] = accq[...]
     gwk_ref[...] = acck[pl.ds(pl.multiple_of(k * 64, 64), 32), :]
     gwv_ref[...] = acck[pl.ds(pl.multiple_of(k * 64 + 32, 32), 32), :]
-    for c in range(4):
+    for c in range(5):
         for d in (1, 3, 2):
             receive(gzr.at[c, d], gz_r.at[c * 4 + d], gz_s.at[c * 4 + d])
-        gi_ref[:, c * 128 : (c + 1) * 128] = (
+        gi_ref[c * 16 : (c + 1) * 16, :] = (
             gys[c, zh].astype(F32)
             + gzr[c, 1].astype(F32)
             + gzr[c, 2].astype(F32)
@@ -505,18 +539,18 @@
     scratch = [
         b(512, 256), b(32, 512), b(32, 512), b(TOK, 256), b(32, TOK), b(32, TOK), b(TOK, 256),
         pltpu.VMEM((1, TOK), jnp.int32), pltpu.VMEM((1, TOK), jnp.int32),
-        b(2, 4, 8, HALF, 128), b(4, 4, 16, 256), f(4, TOK, 64), f(4, TOK, 64), b(256, 256),
-        b(16, TOK, 128), b(16, TOK, 128), f(16, TOK, LANES), f(16, TOK, LANES), b(4, TOK, LANES),
+        b(2, 4, 8, HALF, 128), b(4, 4, 16, 256), f(4, TOK, HEAD), f(4, TOK, HEAD), b(256, 256),
+        b(16, TOK, 128), b(16, TOK, 128), f(16, TOK, LANES), f(16, TOK, LANES), b(16, TOK, LANES), b(16, TOK, LANES),
         b(128, LANES), b(128, LANES), b(LANES, 128), b(LANES, 128),
         b(512, 512), b(128, 512), f(128, LANES),
         b(2, 4, 4, 2, HALF, 128), b(4, 4, 2, HALF, 128), b(4, 4, 2, HALF, 128),
         b(4, 4, 2, HALF, 128), b(4, 2, HALF, 128), b(8, HALF, 128),
         b(4, 4, HALF, 128), b(4, 4, HALF, 128),
         b(2, HALF, 256), b(4, 4, HALF, 512), b(4, 4, HALF, 256), b(4, 4, 2, HALF, 512),
-        b(4, 4, 4, HALF, 128), b(4, 4, 4, HALF, 128), b(4, 4, HALF, 128), b(4, 4, HALF, 128),
+        b(5, 4, 4, 16, 512), b(5, 4, 4, 16, 512), b(5, 4, 16, 512), b(5, 4, 16, 512),
         f(512, 256), f(128, 512), pltpu.SemaphoreType.DMA((10,)),
     ]
-    sizes = [4, 4, 8, 32, 4, 2, 4, 4, 4, 4, 8, 16, 4, 16, 4, 1, 4, 16, 4, 16, 16]
+    sizes = [4, 4, 8, 32, 4, 2, 4, 4, 4, 4, 8, 16, 4, 16, 4, 1, 4, 16, 8, 4, 20, 20]
     for size in sizes:
         scratch += [pltpu.SemaphoreType.DMA((size,)), pltpu.SemaphoreType.DMA((size,))]
     gi, gwq, gwk, gwv = pl.pallas_call(

time: 106 us -> 103 us (0.972)
  Pallas kernels: 106 us -> 102 us
    pallas_call x1, Pallas kernels: 104 us -> 100 us  [shards(): pl.pallas_call(kernel, out_shape=(jax.ShapeDtypeStruct((HALF, 512), BF),...]
where the time goes in v4:
time: 103 us
  Pallas kernels  102 us (99%)
    pallas_call x1, Pallas kernels, shards(): pl.pallas_call(kernel, out_shape=(jax.ShapeDtypeStruct((HALF, 512), BF),...  100 us

profile of v4, /device:TPU:1, one launch (start us, length us, event | category | flops | bytes accessed | tf_op | source)
XLA Modules:
  0.0 102.7 jit_solution(2728373098604147743)
XLA Ops:
  0.6 100.0 %attention_backward.1 = (bf16[80,512]{1,0:T(8,128)(2,1)}, f32[512,256]{1,0:T(8,128)}, f32[32,512]{1,0:T(8,128)}, f32[32,512]{1,0:T(8,128)}) custom-call(bf16[80,512]{1,0:T(8,128)(2,1)} %x_hbm.1, bf16[512,256]{1,0:T(8,128)(2,1)} %wq_hbm.1, bf16[32,512]{1,0:T(8,128)(2,1)} %bitcast.8, bf16[32,512]{1,0:T(8,128)(2,1)} %bitcast.9, bf16[160,256]{1,0:T(8,128)(2,1)} %q_hbm.1, ...), custom_call_target="tpu_custom_call" | custom-call | tf_op jit(solution)/shard_map/attention_backward/pallas_call | solution.py:556
  100.7 2.0 %write_out.1 = (bf16[80,512]{1,0:T(8,128)(2,1)}, f32[512,256]{1,0:T(8,128)}, f32[32,512]{1,0:T(8,128)}, f32[32,512]{1,0:T(8,128)}) custom-call(bf16[80,512]{1,0:T(8,128)(2,1)} %get-tuple-element.12.a, f32[512,256]{1,0:T(8,128)} %get-tuple-element.13.b, f32[32,512]{1,0:T(8,128)} %get-tuple-element.14.c, f32[32,512]{1,0:T(8,128)} %get-tuple-element.15.d), custom_call_target="tpu_custom_call" | custom-call | tf_op jit(solution)/shard_map/write_out/pallas_call | solution.py:577

commit v5 on v4

--- a/solution.py
+++ b/solution.py
@@ -286,7 +286,25 @@
         )
         return 0
 
-    lax.fori_loop(0, 4, score_grads, 0)
+    before = None
+    for d in (2, 1, 3, 0):
+        there = lax.rem(x + d, 4)
+        score_grads(there, 0)
+
+        def grad_step(i, _):
+            b = there * 4 + i
+            dkey = dot(ds[b], qr[...]).astype(BF)
+            dvalue = dot(low[b], orow[...]).astype(BF)
+            for half in range(2):
+                dkp[half, there, i, 0] = dkey[half * HALF : (half + 1) * HALF]
+                dkp[half, there, i, 1] = dvalue[half * HALF : (half + 1) * HALF]
+            return 0
+
+        lax.fori_loop(0, 4, grad_step, 0, unroll=2)
+        send(dkp.at[1 - k, there], dkr.at[there], dc_s.at[d], dc_r.at[d], mate)
+        if before is not None:
+            key_sum(before)
+        before = d
     dquery = dqacc[...].T
     for head in range(2):
         part = dquery[head * TOK : (head + 1) * TOK]
@@ -298,35 +316,13 @@
     send(dqo.at[1 - k], dqg.at[x, zl, :, mine], qm_s.at[0], qm_r.at[0], mate)
     dqg[x, zl, :, mine] = dqo[k]
 
-    before = None
-    for d in (2, 1, 3, 0):
-        there = lax.rem(x + d, 4)
-
-        def grad_step(i, _):
-            b = there * 4 + i
-            dkey = dot(ds[b], qr[...]).astype(BF)
-            dvalue = dot(low[b], orow[...]).astype(BF)
-            for half in range(2):
-                dkp[half, there, i, 0] = dkey[half * HALF : (half + 1) * HALF]
-                dkp[half, there, i, 1] = dvalue[half * HALF : (half + 1) * HALF]
-            return 0
-
-        lax.fori_loop(0, 4, grad_step, 0, unroll=2)
-        send(dkp.at[1 - k, there], dkr.at[there], dc_s.at[d], dc_r.at[d], mate)
-        if before is None:
-            receive(dqg.at[x, zl, :, other], qm_r.at[0], qm_s.at[0])
-            block = dqg.at[x, zl]
-            for e in (2, 1, 3):
-                send(block, block, qz_s.at[e], qz_r.at[e], at_zl(e))
-        else:
-            key_sum(before)
-        before = d
     key_sum(0)
     for d in (2, 1, 3):
         key_send(d, 1)
+    receive(dqg.at[x, zl, :, other], qm_r.at[0], qm_s.at[0])
     block = dqg.at[x, zl]
-    for d in (1, 3):
-        send(block, block, qx_s.at[d * 4], qx_r.at[d * 4], at_x(d))
+    for e in (2, 1, 3):
+        send(block, block, qz_s.at[e], qz_r.at[e], at_zl(e))
 
     rows = pl.ds(pl.multiple_of(k * 64, 64), 64)
     wkv[rows, :] = jnp.concatenate([wk_ref[...], wv_ref[...]], axis=0)
@@ -370,6 +366,9 @@
                 dz_s.at[e * 2 + part], dz_r.at[e * 2 + part], at_run(e),
             )
 
+    block = dqg.at[x, zl]
+    for d in (1, 3):
+        send(block, block, qx_s.at[d * 4], qx_r.at[d * 4], at_x(d))
     for e in (1, 3, 2):
         block = dqg.at[x, lax.rem(zl + 4 - e, 4)]
         receive(block, qz_r.at[e], qz_s.at[e])
@@ -463,6 +462,9 @@
                 gz_s.at[c * 4 + d], gz_r.at[c * 4 + d], at_zh(d),
             )
 
+    for there in range(4):
+        send(dqg.at[there, :, :, other], dqm.at[there], qc_s.at[there], qc_r.at[there], mate)
+        send(gk.at[there], gkm.at[there], pc_s.at[there], pc_r.at[there], mate)
     flying = []
     for c in range(5):
         input_part(c)
@@ -472,9 +474,7 @@
             sent(flying[c - 2])
         flying.append(input_send(c))
 
-    for there in range(4):
-        send(dqg.at[there, :, :, other], dqm.at[there], qc_s.at[there], qc_r.at[there], mate)
-        send(gk.at[there], gkm.at[there], pc_s.at[there], pc_r.at[there], mate)
+    input_sum(1)
     for there in range(4):
         receive(dqm.at[there], qc_r.at[there], qc_s.at[there])
         receive(gkm.at[there], pc_r.at[there], pc_s.at[there])
@@ -497,10 +497,9 @@
         lax.fori_loop(first, last, weight_step, 0)
 
     weight_part(0, 1)
-    for c in range(1, 5):
+    for c in range(2, 5):
         input_sum(c)
-        if c < 4:
-            weight_part(c, c + 1)
+        weight_part(c - 1, c)
     gwq_ref[...] = accq[...]
     gwk_ref[...] = acck[pl.ds(pl.multiple_of(k * 64, 64), 32), :]
     gwv_ref[...] = acck[pl.ds(pl.multiple_of(k * 64 + 32, 32), 32), :]

time: 103 us -> 99 us (0.961)
  Pallas kernels: 102 us -> 97.9 us
    pallas_call x1, Pallas kernels: 100 us -> 95.9 us  [shards(): pl.pallas_call(kernel, out_shape=(jax.ShapeDtypeStruct((HALF, 512), BF),...]
where the time goes in v5:
time: 99 us; the launch traced here: 98.5 us
  Pallas kernels  97.9 us (99%)
    pallas_call x1, Pallas kernels, shards(): pl.pallas_call(kernel, out_shape=(jax.ShapeDtypeStruct((HALF, 512), BF),...  95.9 us
    pallas_call x1, Pallas kernels, shards(): pl.pallas_call(write_out, out_shape=tuple((jax.ShapeDtypeStruct(r.shape,...  1.98 us

profile of v5, /device:TPU:1, one launch (start us, length us, event | category | flops | bytes accessed | tf_op | source)
XLA Modules:
  0.0 98.5 jit_solution(4210355923706789589)
XLA Ops:
  0.6 95.9 %attention_backward.1 = (bf16[80,512]{1,0:T(8,128)(2,1)}, f32[512,256]{1,0:T(8,128)}, f32[32,512]{1,0:T(8,128)}, f32[32,512]{1,0:T(8,128)}) custom-call(bf16[80,512]{1,0:T(8,128)(2,1)} %x_hbm.1, bf16[512,256]{1,0:T(8,128)(2,1)} %wq_hbm.1, bf16[32,512]{1,0:T(8,128)(2,1)} %bitcast.8, bf16[32,512]{1,0:T(8,128)(2,1)} %bitcast.9, bf16[160,256]{1,0:T(8,128)(2,1)} %q_hbm.1, ...), custom_call_target="tpu_custom_call" | custom-call | tf_op jit(solution)/shard_map/attention_backward/pallas_call | solution.py:555
  96.6 2.0 %write_out.1 = (bf16[80,512]{1,0:T(8,128)(2,1)}, f32[512,256]{1,0:T(8,128)}, f32[32,512]{1,0:T(8,128)}, f32[32,512]{1,0:T(8,128)}) custom-call(bf16[80,512]{1,0:T(8,128)(2,1)} %get-tuple-element.12.a, f32[512,256]{1,0:T(8,128)} %get-tuple-element.13.b, f32[32,512]{1,0:T(8,128)} %get-tuple-element.14.c, f32[32,512]{1,0:T(8,128)} %get-tuple-element.15.d), custom_call_target="tpu_custom_call" | custom-call | tf_op jit(solution)/shard_map/write_out/pallas_call | solution.py:576

commit v6 on v5

--- a/solution.py
+++ b/solution.py
@@ -210,18 +210,6 @@
 
     receive(kv.at[1 - k, x], kc_r.at[0], kc_s.at[0])
     peak = products(x, jnp.full((1, LANES), -1e30, F32))
-    place = lax.broadcasted_iota(jnp.int32, (HEAD, TOK), 0)
-    freq = jnp.exp(-(2.0 * lax.rem(place, 64).astype(F32) / HEAD) * math.log(ROPE_BASE))
-    sign = jnp.where(place < 64, 1.0, -1.0)
-
-    def tables(i, _):
-        facts = meta[x, i].astype(F32)
-        angle = (facts[1:2, 0:TOK] * 64.0 + facts[2:3, 0:TOK]) * freq
-        cosine[i] = jnp.cos(angle).T
-        sine[i] = (jnp.sin(angle) * sign).T
-        return 0
-
-    lax.fori_loop(0, 4, tables, 0)
     def pass_on(d):
         there = lax.rem(x + 4 - d, 4)
         if d == 2:
@@ -235,6 +223,18 @@
 
     pass_on(1)
     pass_on(3)
+    place = lax.broadcasted_iota(jnp.int32, (HEAD // 2, TOK), 0).astype(F32)
+    freq = jnp.exp(-(2.0 * place / HEAD) * math.log(ROPE_BASE))
+
+    def tables(i, _):
+        facts = meta[x, i].astype(F32)
+        angle = (facts[1:2, 0:TOK] * 64.0 + facts[2:3, 0:TOK]) * freq
+        cos, sin = jnp.cos(angle), jnp.sin(angle)
+        cosine[i] = jnp.concatenate([cos, cos], axis=0).T
+        sine[i] = jnp.concatenate([sin, -sin], axis=0).T
+        return 0
+
+    lax.fori_loop(0, 4, tables, 0)
     for d in (1, 3, 2):
         there = lax.rem(x + 4 - d, 4)
         receive(kv.at[1 - k, there], kc_r.at[d], kc_s.at[d])

time: 99 us -> 98.7 us (level)
  the two profiles are of different devices: /device:TPU:1 before, /device:TPU:32 now
where the time goes in v6:
time: 98.7 us; the launch traced here: 98.5 us
  Pallas kernels  97.9 us (99%)
    pallas_call x1, Pallas kernels, shards(): pl.pallas_call(kernel, out_shape=(jax.ShapeDtypeStruct((HALF, 512), BF),...  95.9 us
    pallas_call x1, Pallas kernels, shards(): pl.pallas_call(write_out, out_shape=tuple((jax.ShapeDtypeStruct(r.shape,...  1.98 us

profile of v6, /device:TPU:32, one launch (start us, length us, event | category | flops | bytes accessed | tf_op | source)
XLA Modules:
  0.0 98.5 jit_solution(4594109512251855539)
XLA Ops:
  0.6 95.9 %attention_backward.1 = (bf16[80,512]{1,0:T(8,128)(2,1)}, f32[512,256]{1,0:T(8,128)}, f32[32,512]{1,0:T(8,128)}, f32[32,512]{1,0:T(8,128)}) custom-call(bf16[80,512]{1,0:T(8,128)(2,1)} %x_hbm.1, bf16[512,256]{1,0:T(8,128)(2,1)} %wq_hbm.1, bf16[32,512]{1,0:T(8,128)(2,1)} %bitcast.8, bf16[32,512]{1,0:T(8,128)(2,1)} %bitcast.9, bf16[160,256]{1,0:T(8,128)(2,1)} %q_hbm.1, ...), custom_call_target="tpu_custom_call" | custom-call | tf_op jit(solution)/shard_map/attention_backward/pallas_call | solution.py:555
  96.5 2.0 %write_out.1 = (bf16[80,512]{1,0:T(8,128)(2,1)}, f32[512,256]{1,0:T(8,128)}, f32[32,512]{1,0:T(8,128)}, f32[32,512]{1,0:T(8,128)}) custom-call(bf16[80,512]{1,0:T(8,128)(2,1)} %get-tuple-element.12.a, f32[512,256]{1,0:T(8,128)} %get-tuple-element.13.b, f32[32,512]{1,0:T(8,128)} %get-tuple-element.14.c, f32[32,512]{1,0:T(8,128)} %get-tuple-element.15.d), custom_call_target="tpu_custom_call" | custom-call | tf_op jit(solution)/shard_map/write_out/pallas_call | solution.py:576
